TPU v7x, 512 devices: a whole 4x4x16 slice. The times are simulated.
512 devices in a mesh: expert: 16 (over x, y), fsdp: 32 (over z, core).
Axes of the slice: x: 4, y: 4, z: 16, core: 2. Of those that a mesh axis runs over, the one named last changes fastest.
Arguments:
- tokens: bfloat16 [4096, 4096], P('fsdp', 'expert'), may hold values from -6 to 6
- segment_ids: int32 [4096], replicated, may hold values from 0 to 3, never falling along the last dimension, each value on 1 to 2048 neighbouring positions
- w_in_x: bfloat16 [4096, 8192], P('fsdp', 'expert'), may hold values from -0.09375 to 0.09375
- w_in_z: bfloat16 [4096, 8192], P('fsdp', 'expert'), may hold values from -0.09375 to 0.09375
- conv_weight: float32 [4, 8192], P(None, 'expert'), may hold values from -3 to 3
- conv_bias: float32 [8192], P('expert'), may hold values from -3 to 3
- w_xproj: bfloat16 [8192, 288], P('expert'), may hold values from -0.0625 to 0.0625
- w_dt: bfloat16 [256, 8192], P(None, 'expert'), may hold values from -0.375 to 0.375
- dt_bias: float32 [8192], P('expert'), may hold values from -4 to 1
- a_rate: float32 [8192, 16], P('expert'), may hold values from 0.002 to 2
- d_skip: float32 [8192], P('expert'), may hold values from 0.5 to 1.5
- w_out: bfloat16 [8192, 4096], P('expert', 'fsdp'), may hold values from -0.0625 to 0.0625
Outputs:
- mixed: bfloat16 [4096, 4096], P('fsdp', 'expert')
Inputs may be any that keep to these rules, and one draw needn't show every extreme that they name: `segment_ids`: document ids never fall along the sequence; each document has at most 2048 tokens, and one has exactly that many.
All inputs are finite; a program needn't handle non-finite values.
Results may differ from a plain program's by a relative error of at most 0.03.
Values may be sent and summed in bfloat16 or wider, within the bound.
A program may use at most 64 MiB of HBM per device.

v0:
```python
import jax
import jax.numpy as jnp
from jax import lax
from jax.sharding import PartitionSpec as P


def passed_along(block, axis, distance):
    devices = range(lax.axis_size(axis))
    route = [(i - distance, i) for i in devices if i - distance in devices]
    return lax.ppermute(block, axis, route)


def entering(x, axis, join, neutral):
    place = lax.axis_index(axis)
    gathered = jax.tree.map(
        lambda a, kind: lax.all_gather(a.astype(kind), axis), x, (jnp.bfloat16, jnp.bfloat16)
    )
    state = jax.tree.map(lambda a, e: jnp.zeros_like(a) + jnp.asarray(e, a.dtype), x, neutral)

    def one(step, state):
        return join(
            state,
            jax.tree.map(
                lambda a, own: lax.dynamic_index_in_dim(a, step, 0, False).astype(own.dtype),
                gathered,
                x,
            ),
        )

    return lax.fori_loop(0, place, one, state)


def local(
    tokens,
    segment_ids,
    w_in_x,
    w_in_z,
    conv_weight,
    conv_bias,
    w_xproj,
    w_dt,
    dt_bias,
    a_rate,
    d_skip,
    w_out,
):
    features = lax.all_gather(tokens, "expert", axis=1, tiled=True)
    row_count = features.shape[0]
    channels = w_in_x.shape[1]
    zero_block = jnp.zeros((row_count, channels), jnp.float32)

    def add_rows(weight_piece):
        return jnp.dot(features, weight_piece, preferred_element_type=jnp.float32)

    x_sum = add_rows(lax.all_gather(w_in_x, "fsdp", axis=0, tiled=True))
    z_sum = add_rows(lax.all_gather(w_in_z, "fsdp", axis=0, tiled=True))
    x_in = x_sum.astype(jnp.bfloat16)
    z_in = z_sum.astype(jnp.bfloat16)
    kernel = conv_weight.shape[0]
    conv_rim = passed_along(x_in[row_count - (kernel - 1) :], "fsdp", 1)
    extended = jnp.concatenate([conv_rim, x_in], 0).astype(jnp.float32)
    first_row = lax.axis_index("fsdp") * row_count
    padded_ids = jnp.concatenate([jnp.full((kernel - 1,), -1, jnp.int32), segment_ids], 0)
    window_ids = lax.dynamic_slice_in_dim(padded_ids, first_row, row_count + kernel - 1)
    own_ids = window_ids[kernel - 1 :]
    conv_out = zero_block + conv_bias[None, :]
    for offset in range(kernel):
        same_doc = (window_ids[offset : offset + row_count] == own_ids).astype(jnp.float32)
        conv_out = (
            conv_out
            + conv_weight[offset][None, :]
            * extended[offset : offset + row_count]
            * same_doc[:, None]
        )
    x_act = jax.nn.silu(conv_out).astype(jnp.bfloat16)
    partial_proj = jnp.dot(x_act, w_xproj, preferred_element_type=jnp.float32)
    projected = lax.psum(partial_proj.astype(jnp.bfloat16), "expert").astype(jnp.float32)
    rank_size = w_dt.shape[0]
    state_size = a_rate.shape[1]
    dt_low = projected[:, :rank_size].astype(jnp.bfloat16)
    b_in = projected[:, rank_size : rank_size + state_size]
    c_out = projected[:, rank_size + state_size :]
    delta = jax.nn.softplus(
        jnp.dot(dt_low, w_dt, preferred_element_type=jnp.float32) + dt_bias[None, :]
    )
    keep_mask = (
        window_ids[kernel - 1 :] == window_ids[kernel - 2 : row_count + kernel - 2]
    ).astype(jnp.float32)
    x_float = x_act.astype(jnp.float32)

    def scan_step(hidden_state, inputs):
        delta_t, x_t, b_t, c_t, keep_t = inputs
        decay = jnp.exp(-delta_t[:, None] * a_rate) * keep_t
        hidden_state = decay * hidden_state + (delta_t * x_t)[:, None] * b_t[None, :]
        return (hidden_state, jnp.sum(hidden_state * c_t[None, :], axis=1))

    zero_state = jnp.zeros((channels, state_size), jnp.float32)
    unit_state = jnp.ones((channels, state_size), jnp.float32)
    state_end, outputs = lax.scan(
        scan_step, zero_state, (delta, x_float, b_in, c_out, keep_mask), unroll=8
    )
    delta_total = jnp.cumsum(delta, axis=0)
    linked = (own_ids == window_ids[kernel - 2]).astype(jnp.float32)
    prod_end = jnp.exp(-delta_total[row_count - 1][:, None] * a_rate) * linked[row_count - 1]

    def combine(earlier, latter):
        return (earlier[0] * latter[0], latter[0] * earlier[1] + latter[1])

    prod_before, state_start = entering(
        (prod_end, state_end), "fsdp", combine, (unit_state, zero_state)
    )
    weighted_start = state_start[None, :, :] * c_out[:, None, :]
    carried_in = jnp.sum(
        jnp.exp(-delta_total[:, :, None] * a_rate[None, :, :]) * weighted_start, axis=2
    )
    outputs = outputs + carried_in * linked[:, None]
    scanned = outputs + d_skip[None, :] * x_float
    gated = (scanned * jax.nn.silu(z_in.astype(jnp.float32))).astype(jnp.bfloat16)
    partials = jnp.dot(
        gated, lax.all_gather(w_out, "fsdp", axis=1, tiled=True), preferred_element_type=jnp.float32
    )
    mixer_out = lax.psum_scatter(
        partials.astype(jnp.bfloat16), "expert", scatter_dimension=1, tiled=True
    )
    return mixer_out


def solution(mesh):
    placed = (
        P("fsdp", "expert"),
        P(),
        P("fsdp", "expert"),
        P("fsdp", "expert"),
        P(None, "expert"),
        P("expert"),
        P("expert", None),
        P(None, "expert"),
        P("expert"),
        P("expert", None),
        P("expert"),
        P("expert", "fsdp"),
    )
    return jax.shard_map(
        local, mesh=mesh, in_specs=placed, out_specs=P("fsdp", "expert"), check_vma=False
    )
```

profile of v0, /device:TPU:1, one launch (start us, length us, event | category | flops | bytes accessed | tf_op | source)
XLA Modules:
  0.0 573.4 jit_solution(9658341684705161423)
XLA Ops:
  10.4 62.6 %all-gather.7.cloned.1.call-done = bf16[128,4096]{1,0:T(8,128)(2,1)} async-done(((bf16[128,256]{1,0:T(8,128)(2,1)}), bf16[128,4096]{1,0:T(8,128)(2,1)}) %all-gather.7.cloned.1.call-update) | async-done | bytes 1048592 | tf_op jit(solution)/shard_map/all_gather | solution.py:47
  73.0 77.2 %all-gather.9.cloned.1.call-done = bf16[4096,512]{1,0:T(8,128)(2,1)} async-done(((bf16[128,512]{1,0:T(8,128)(2,1)}), bf16[4096,512]{1,0:T(8,128)(2,1)}) %all-gather.9.cloned.1.call-update) | async-done | bytes 4194320 | tf_op jit(solution)/shard_map/all_gather | solution.py:55
  150.1 3.2 convolution_convert_fusion.2
  153.4 3.6 collective-permute-start
  161.0 106.5 %all-reduce.3.cloned.1.call-done = bf16[128,288]{0,1:T(8,128)(2,1)} async-done(((bf16[128,288]{0,1:T(8,128)(2,1)}), bf16[128,288]{0,1:T(8,128)(2,1)}) %all-reduce.3.cloned.1.call-update) | async-done | bytes 73744 | tf_op jit(solution)/shard_map/psum | solution.py:77
  269.7 141.0 %while.26 = (s32[]{:T(128)}, f32[512,16]{0,1:T(8,128)S(1)}, f32[16,8,512]{2,1,0:T(8,128)S(1)}, f32[16,8,512]{2,1,0:T(8,128)S(1)}, f32[512,16]{0,1:T(8,128)S(1)},...) while((s32[]{:T(128)}, f32[512,16]{0,1:T(8,128)S(1)}, ...), condition=%wide.region_10.11_spmd.clone, body=%wide.region_1.10_spmd.clone.sunk | while | flops 643082 | bytes 661216 | solution.py:99
  270.5 5.2 multiply_reduce_fusion.12
  279.3 5.2 multiply_reduce_fusion.12
  288.1 5.2 multiply_reduce_fusion.12
  296.9 5.2 multiply_reduce_fusion.12
  305.7 5.2 multiply_reduce_fusion.12
  314.5 5.2 multiply_reduce_fusion.12
  323.3 5.2 multiply_reduce_fusion.12
  329.9 1.4 multiply_reduce_fusion.13
  332.2 5.2 multiply_reduce_fusion.12
  338.7 1.4 multiply_reduce_fusion.13
  341.0 5.2 multiply_reduce_fusion.12
  347.5 1.4 multiply_reduce_fusion.13
  349.8 5.2 multiply_reduce_fusion.12
  356.3 1.4 multiply_reduce_fusion.13
  358.6 5.2 multiply_reduce_fusion.12
  365.1 1.4 multiply_reduce_fusion.13
  367.4 5.2 multiply_reduce_fusion.12
  376.2 5.2 multiply_reduce_fusion.12
  385.0 5.2 multiply_reduce_fusion.12
  393.8 5.2 multiply_reduce_fusion.12
  402.6 5.2 multiply_reduce_fusion.12
  409.2 1.4 multiply_reduce_fusion.13
  410.7 35.0 %all-gather.1 = bf16[16384,16]{0,1:T(8,128)(2,1)S(1)} all-gather(bf16[512,16]{0,1:T(8,128)(2,1)S(1)} %convert_element_type.86), channel_id=3, replica_groups=mesh['expert'=16,'fsdp'=32] {'fsdp'}, dimensions={0}, use_global_device_ids=true | all-gather | bytes 540672 | tf_op jit(solution)/shard_map/all_gather | solution.py:16
  446.8 29.4 %all-gather = bf16[16384,16]{0,1:T(8,128)(2,1)S(1)} all-gather(bf16[512,16]{0,1:T(8,128)(2,1)S(1)} %multiply_convert_fusion.1), channel_id=2, replica_groups=mesh['expert'=16,'fsdp'=32] {'fsdp'}, dimensions={0}, use_global_device_ids=true | all-gather | bytes 540672 | tf_op jit(solution)/shard_map/all_gather | solution.py:16
  477.7 6.0 %convolution_convert_fusion = bf16[128,4096]{1,0:T(8,128)(2,1)} fusion(bf16[512,4096]{1,0:T(8,128)(2,1)} %all-gather.13.cloned.1.call-done, bf16[128,512]{1,0:T(8,128)(2,1)S(1)} %get-tuple-element.213, f32[16,8,512]{2,1,0:T(8,128)S(1)} %get-tuple-element.97, bf16[128,4096]{1,0:T(8,128)(2,1)S(1)} %copy-done.2, ...), kind=kOutput, calls=%fused_computation.71 | convolution fusion | flops 1075118080 | bytes 11143680 | tf_op jit(solution)/shard_map/dot_general | solution.py:119
  483.7 82.9 %reduce-scatter.2.cloned.1.call-done = bf16[128,256]{1,0:T(8,128)(2,1)} async-done(((bf16[128,4096]{1,0:T(8,128)(2,1)}), bf16[128,256]{1,0:T(8,128)(2,1)}) %reduce-scatter.2.cloned.1.call-update) | async-done | bytes 65552 | tf_op jit(solution)/shard_map/reduce_scatter | solution.py:122
  (226 shorter events, 61.2 us)
Async XLA Ops:
  6.5 151.6 %copy-start = (bf16[512,288]{0,1:T(8,128)(2,1)S(1)}, bf16[512,288]{0,1:T(8,128)(2,1)}, u32[]{:S(2)}) copy-start(bf16[512,288]{0,1:T(8,128)(2,1)} %param.22) | copy-start | bytes 884740
  6.5 151.3 %copy-start.3 = (f32[512]{0:T(512)S(1)}, f32[512]{0:T(512)}, u32[]{:S(2)}) copy-start(f32[512]{0:T(512)} %param.21) | copy-start | bytes 6148
  6.5 66.4 %all-gather.7.cloned.1.call-start = ((), (), s32[]{:S(2)}) async-start(), calls=%async_computation.1 | async-start | bytes 1114112 | tf_op jit(solution)/shard_map/all_gather | solution.py:47
  7.3 142.9 %all-gather.9.cloned.1.call-start = ((), (), s32[]{:S(2)}) async-start(), calls=%async_computation.2 | async-start | bytes 4325376 | tf_op jit(solution)/shard_map/all_gather | solution.py:55
  8.0 260.4 %copy-start.5 = (bf16[256,512]{1,0:T(8,128)(2,1)S(1)}, bf16[256,512]{1,0:T(8,128)(2,1)}, u32[]{:S(2)}) copy-start(bf16[256,512]{1,0:T(8,128)(2,1)} %param.23) | copy-start | bytes 786436
  8.0 260.4 %copy-start.6 = (f32[512]{0:T(512)S(1)}, f32[512]{0:T(512)}, u32[]{:S(2)}) copy-start(f32[512]{0:T(512)} %param.24) | copy-start | bytes 6148
  8.0 259.5 %all-reduce.3.cloned.1.call-start = ((), (), s32[]{:S(2)}) async-start(), calls=%async_computation.3 | async-start | bytes 147456 | tf_op jit(solution)/shard_map/psum | solution.py:77
  10.4 259.3 %copy-start.1 = (f32[512,16]{0,1:T(8,128)S(1)}, f32[512,16]{0,1:T(8,128)}, u32[]{:S(2)}) copy-start(f32[512,16]{0,1:T(8,128)} %param.25) | copy-start | bytes 98308
  153.4 4.4 collective-permute-start
  159.0 318.6 %all-gather.11.cloned.1.call-start = ((), (), s32[]{:S(2)}) async-start(), calls=%async_computation.4 | async-start | bytes 4325376 | tf_op jit(solution)/shard_map/all_gather | solution.py:56
  159.6 318.1 %all-gather.13.cloned.1.call-start = ((), (), s32[]{:S(2)}) async-start(), calls=%async_computation.5 | async-start | bytes 4325376 | tf_op jit(solution)/shard_map/all_gather | solution.py:120
  160.2 406.4 %reduce-scatter.2.cloned.1.call-start = ((), (), s32[]{:S(2)}) async-start(), calls=%async_computation.6 | async-start | bytes 1114112 | tf_op jit(solution)/shard_map/reduce_scatter | solution.py:122
  410.6 67.0 %copy-start.2 = (bf16[128,4096]{1,0:T(8,128)(2,1)S(1)}, bf16[128,4096]{1,0:T(8,128)(2,1)}, u32[]{:S(2)}) copy-start(bf16[128,4096]{1,0:T(8,128)(2,1)} %all-gather.7.cloned.1.call-done) | copy-start | bytes 3145732
  410.6 67.0 %copy-start.4 = (f32[512]{0:T(512)S(1)}, f32[512]{0:T(512)}, u32[]{:S(2)}) copy-start(f32[512]{0:T(512)} %param.26) | copy-start | bytes 6148
Sparse Core Ops, SparseCore 0:
  10.3 62.5 all-gather.6
  75.1 75.0 all-gather.8
  159.2 108.3 all-reduce.2
  269.8 75.8 all-gather.10
  347.7 76.8 all-gather.12
  483.8 82.7 reduce-scatter.1
where the time goes:
time: 576 us; the launch traced here: 573 us
  waiting for transfers between devices  332 us (58%)
  other arithmetic  131 us (23%)
  blocking collectives  64.4 us (11%)
  local copies, waits for them, and re-layouts  16.4 us (3%)
  between operations  13.7 us (2%)
  matrix products  11.2 us (2%)
    reduce_sum x48, other arithmetic, scan_step(): return (hidden_state, jnp.sum(hidden_state * c_t[None, :], axis=1))  127 us
    psum x1, waiting for transfers between devices, local(): lax.psum(partial_proj.astype(jnp.bfloat16), 'expert').astype(jnp.float32)  107 us
    reduce_scatter x1, waiting for transfers between devices, local(): lax.psum_scatter(partials.astype(jnp.bfloat16), 'expert', scatter_dimensi...  82.9 us
    all_gather x1, waiting for transfers between devices, local(): x_sum = add_rows(lax.all_gather(w_in_x, 'fsdp', axis=0, tiled=True))  77.2 us
    all_gather x2, blocking collectives, entering(): lax.all_gather(a.astype(kind), axis)  64.4 us
    all_gather x1, waiting for transfers between devices, local(): features = lax.all_gather(tokens, 'expert', axis=1, tiled=True)  62.6 us
  transfers between devices with their start and end apart: 7, of which 4 were waited for; matrix products, arithmetic and copies ran while one was open for 26% of the time, Pallas kernels for 0%

commit v1 on v0

v1 whole, which is shorter than its diff:
```python
import functools
import math

import jax
import jax.numpy as jnp
from jax import lax
from jax.experimental import pallas as pl
from jax.experimental.pallas import tpu as pltpu
from jax.sharding import PartitionSpec as P

F32 = jnp.float32
BF16 = jnp.bfloat16
FAR = 1e30
LOG2E = 1.0 / math.log(2.0)
MESH = pl.DeviceIdType.MESH


def silu(v):
    return v * jax.nn.sigmoid(v)


def dot(a, b):
    return jnp.dot(a, b, preferred_element_type=F32)


def kernel(
    sizes,
    tok, wx, wz, wo, conv_w, conv_b, wxp, wdt, dt_bias, rates, d_skip, masks,
    out,
    TOK, WX, WZ, WO, AX, AZ, XP, HALO, ZS, XA, PP, PA, PS, RB, PR,
    DD, DX, SC, Y, HE, PE, KM, KR, G, XS, XR, MO, OS, RO,
    local_sem, pair_s, pair_r, tok_s, tok_r, fwd_s, fwd_r, ring_s, ring_r,
    halo_s, halo_r, half_s, half_r, sum_s, sum_r, all_s, all_r,
    state_s, state_r, swap_s, swap_r, out_s, out_r,
):
    NE, NZ, TL, KR_, CH, OC, R, N = sizes
    T, J, H = 2 * TL, TL // 4, NZ // 2
    PW = R + 128
    hops = [1, 1]
    while sum(hops) < H:
        hops.append(2 * hops[-1])
    e = lax.axis_index("expert")
    f = lax.axis_index("fsdp")
    z = lax.div(f, 2)
    c = lax.rem(f, 2)
    o = 1 - c

    def zmod(v):
        return lax.rem(v + 2 * NZ, NZ)

    def emod(v):
        return lax.rem(v + 2 * NE, NE)

    def at(e_, z_, c_):
        return (e_, 2 * z_ + c_)

    def remote(src, dst, ss, rs, dev):
        return pltpu.make_async_remote_copy(
            src_ref=src, dst_ref=dst, send_sem=ss, recv_sem=rs, device_id=dev, device_id_type=MESH
        )

    def span(i, n, unit=None):
        return pl.ds(pl.multiple_of(i * n, n), n)

    partner = at(e, z, o)
    me = at(e, z, c)

    own = [
        pltpu.make_async_copy(wx.at[:, span(c, CH)], WX.at[z, span(c, KR_)], local_sem.at[0]),
        pltpu.make_async_copy(wz.at[:, span(c, CH)], WZ.at[z, span(c, KR_)], local_sem.at[1]),
        pltpu.make_async_copy(wo.at[span(c, CH)], WO.at[z, :, span(c, OC)], local_sem.at[2]),
        pltpu.make_async_copy(tok, TOK.at[e, span(c, TL)], local_sem.at[3]),
    ]
    for copy in own:
        copy.start()

    barrier = pltpu.get_barrier_semaphore()
    friends = [partner]
    for d in sorted(set(hops)):
        friends += [at(e, zmod(z + d), c), at(e, zmod(z - d), c)]
    for dev in friends:
        pl.semaphore_signal(barrier, inc=1, device_id=dev, device_id_type=MESH)

    def greet(k, _):
        pl.semaphore_signal(
            barrier, inc=1, device_id=at(emod(e + k), z, c), device_id_type=MESH
        )
        return 0

    lax.fori_loop(1, NE, greet, 0)
    pl.semaphore_wait(barrier, len(friends) + NE - 1)

    pairs = [
        remote(wx.at[:, span(o, CH)], WX.at[z, span(c, KR_)], pair_s.at[0], pair_r.at[0], partner),
        remote(wz.at[:, span(o, CH)], WZ.at[z, span(c, KR_)], pair_s.at[1], pair_r.at[1], partner),
        remote(wo.at[span(o, CH)], WO.at[z, :, span(c, OC)], pair_s.at[2], pair_r.at[2], partner),
    ]
    pairs_in = [
        remote(wx.at[:, span(o, CH)], WX.at[z, span(o, KR_)], pair_s.at[0], pair_r.at[0], partner),
        remote(wz.at[:, span(o, CH)], WZ.at[z, span(o, KR_)], pair_s.at[1], pair_r.at[1], partner),
        remote(wo.at[span(o, CH)], WO.at[z, :, span(o, OC)], pair_s.at[2], pair_r.at[2], partner),
    ]
    for copy in pairs:
        copy.start()

    def tok_send(k):
        return remote(
            tok, TOK.at[e, span(c, TL)], tok_s.at[k], tok_r.at[k], at(emod(e + k), z, c)
        )

    def tok_in(k):
        return remote(
            tok, TOK.at[emod(e - k), span(c, TL)], tok_s.at[k], tok_r.at[k], partner
        )

    def tok_fwd(k):
        b = emod(e - k)
        return remote(
            TOK.at[b, span(c, TL)], TOK.at[b, span(c, TL)], fwd_s.at[k], fwd_r.at[k], partner
        )

    def tok_fwd_in(k):
        b = emod(e - k)
        return remote(
            TOK.at[b, span(o, TL)], TOK.at[b, span(o, TL)], fwd_s.at[k], fwd_r.at[k], partner
        )

    def each(lo, hi, fn):
        def body(k, _):
            fn(k)
            return 0

        lax.fori_loop(lo, hi, body, 0)

    each(1, NE, lambda k: tok_send(k).start())

    stacks = [WX, WZ, WO]

    def hop(p, d, s):
        sign = 1 - 2 * d
        block = zmod(z - sign * (s - 1))
        return remote(
            stacks[p].at[block], stacks[p].at[block],
            ring_s.at[p, d, s], ring_r.at[p, d, s], at(e, zmod(z + sign), c),
        )

    def arrive(p, d, s):
        sign = 1 - 2 * d
        block = zmod(z - sign * s)
        remote(
            stacks[p].at[block], stacks[p].at[block],
            ring_s.at[p, d, s], ring_r.at[p, d, s], at(e, zmod(z + sign), c),
        ).wait_recv()

    def add(block, first=False):
        t = TOK[block]
        if first:
            AX[...] = dot(t, WX[block])
            AZ[...] = dot(t, WZ[block])
        else:
            AX[...] += dot(t, WX[block])
            AZ[...] += dot(t, WZ[block])

    for p in (0, 1):
        own[p].wait()
        pairs_in[p].wait_recv()
        hop(p, 0, 1).start()
        hop(p, 1, 1).start()
    own[3].wait()
    tok_fwd(0).start()

    done = 0
    for s in range(1, H):
        for p in (0, 1):
            for d in (0, 1):
                arrive(p, d, s)
                if s < H - 1 or p == d:
                    hop(p, d, s + 1).start()
        if s == H - 1:
            own[2].wait()
            pairs_in[2].wait_recv()
            hop(2, 0, 1).start()
            hop(2, 1, 1).start()
        if s == 1:

            def relay(k):
                tok_in(k).wait_recv()
                tok_fwd(k).start()

            each(1, NE, relay)
        if s == min(2, H - 1):
            each(0, NE, lambda k: tok_fwd_in(k).wait_recv())
            add(z, first=True)
        if s > 2:
            add(zmod(z - (s - 2)))
            add(zmod(z + (s - 2)))
            done = s - 2
    for s in range(done + 1, H):
        add(zmod(z - s))
        add(zmod(z + s))
    arrive(0, 0, H)
    arrive(1, 1, H)
    add(zmod(z + H))

    def pump(s):
        if s < H:
            arrive(2, 0, s)
            hop(2, 0, s + 1).start()
            arrive(2, 1, s)
            if s < H - 1:
                hop(2, 1, s + 1).start()
        elif s == H:
            arrive(2, 0, s)

    row = lax.broadcasted_iota(jnp.int32, (T, T), 0)
    col = lax.broadcasted_iota(jnp.int32, (T, T), 1)
    perm = (col == lax.rem(row, 8) * J + lax.div(row, 8)).astype(F32).astype(BF16)
    XP[...] = dot(perm, AX[...].astype(BF16))
    rim = XP.at[pl.ds((J - 3) * 8, 24)]
    halo = remote(rim, HALO, halo_s, halo_r, at(e, zmod(z + 1), c))
    halo.start()
    ZS[...] = silu(dot(perm, AZ[...].astype(BF16)))
    pump(1)
    halo.wait_recv()
    lane_c = span(c, CH)
    top = lax.broadcasted_iota(jnp.int32, (8, CH), 0) == 0
    early = []
    for i in range(3):
        mine = pltpu.roll(XP[(J - 3 + i) * 8 : (J - 2 + i) * 8], 1, 0)
        theirs = pltpu.roll(HALO[i * 8 : (i + 1) * 8], 1, 0)
        early.append(jnp.where(top, theirs, mine))
    ext = jnp.concatenate(early + [XP[...]], 0)
    conv = conv_b[:, lane_c] + conv_w[3:4, lane_c] * ext[24:]
    for k in range(1, 4):
        conv += conv_w[3 - k : 4 - k, lane_c] * ext[24 - 8 * k : 24 - 8 * k + T] * masks[:, k - 1 : k]
    x_act = silu(conv).astype(BF16)
    XA[...] = x_act.astype(F32)
    PP[...] = dot(x_act, wxp[span(c, CH), :])

    half = remote(PP.at[span(o, TL)], PA, half_s.at[0], half_r.at[0], partner)
    half.start()
    pump(2)
    half.wait_recv()
    PS[...] = PP[span(c, TL), :] + PA[...]

    def sum_send(k):
        return remote(
            PS.at[span(emod(e + k), 8)], RB.at[k], sum_s.at[k], sum_r.at[k], at(emod(e + k), z, c)
        )

    each(1, NE, lambda k: sum_send(k).start())
    pump(3)
    each(1, NE, lambda k: sum_send(k).wait_recv())
    total = PS[span(e, 8), :]
    for k in range(1, NE):
        total += RB[k]
    eighth = pl.ds(pl.multiple_of(c * TL + e * 8, 8), 8)
    PR[eighth, :] = total

    def all_send(k):
        return remote(
            PR.at[eighth], PR.at[eighth], all_s.at[k], all_r.at[k], at(emod(e + k), z, c)
        )

    def all_in(k):
        theirs = pl.ds(pl.multiple_of(c * TL + emod(e - k) * 8, 8), 8)
        return remote(PR.at[theirs], PR.at[theirs], all_s.at[k], all_r.at[k], partner)

    each(1, NE, lambda k: all_send(k).start())
    pump(4)
    each(1, NE, lambda k: all_in(k).wait_recv())
    rest = remote(PR.at[span(c, TL)], PR.at[span(c, TL)], half_s.at[1], half_r.at[1], partner)
    rest_in = remote(PR.at[span(o, TL)], PR.at[span(o, TL)], half_s.at[1], half_r.at[1], partner)
    rest.start()
    pump(5)
    rest_in.wait_recv()

    delta = dot(PR[:, :R].astype(BF16), wdt[:, lane_c]) + dt_bias[:, lane_c]
    delta = jnp.maximum(delta, 0.0) + jnp.log1p(jnp.exp(-jnp.abs(delta)))
    DX[...] = delta * XA[...]
    DD[...] = delta + (1.0 - masks[:, 0:1]) * FAR

    slope = [rates[n : n + 1, lane_c] * (-LOG2E) for n in range(N)]

    def forward(j, carry):
        hs, reach = carry
        r = pl.ds(pl.multiple_of(j * 8, 8), 8)
        dd, dx, bc = DD[r, :], DX[r, :], PR[r, R : R + 128]
        reach = reach + dd
        SC[r, :] = reach
        y = jnp.zeros((8, CH), F32)
        later = []
        for n in range(N):
            h = jnp.exp2(dd * slope[n]) * hs[n] + dx * bc[:, n : n + 1]
            y = y + h * bc[:, N + n : N + n + 1]
            later.append(h)
        Y[r, :] = y
        return later, reach

    zero = jnp.zeros((8, CH), F32)
    ends, reach = lax.fori_loop(0, J, forward, ([zero] * N, zero))
    sub = lax.broadcasted_iota(jnp.int32, (8, CH), 0)
    for n in range(N):
        h, p = ends[n], jnp.exp2(reach * slope[n])
        for d in (1, 2, 4):
            before = sub >= d
            h = h + p * jnp.where(before, pltpu.roll(h, d, 0), 0.0)
            p = p * jnp.where(before, pltpu.roll(p, d, 0), 1.0)
        KM[0, n : n + 1, :] = h[7:8]
        HE[n] = jnp.where(top, 0.0, pltpu.roll(h, 1, 0))
        PE[n] = jnp.where(top, 1.0, pltpu.roll(p, 1, 0))
    KM[0, N : N + 8, :] = jnp.broadcast_to(jnp.sum(reach, axis=0, keepdims=True), (8, CH))

    steep = rates[:, lane_c] * (-LOG2E)

    def state_send(i):
        return remote(
            KM.at[i], KR.at[i], state_s.at[i], state_r.at[i], at(e, zmod(z + hops[i]), c)
        )

    for i in range(len(hops)):
        state_send(i).start()
        pump(6 + i)
        state_send(i).wait_recv()
        if i == 0:
            KM[1] = KR[0]
        else:
            decay = jnp.exp2(KM[i, N : N + 1, :] * steep)
            entering = decay * KR[i, :N, :] + KM[i, :N, :]
            KM[i + 1, :N, :] = entering
            KM[i + 1, N : N + 8, :] = KM[i, N : N + 8, :] + KR[i, N : N + 8, :]
    for s in range(6 + len(hops), H + 1):
        pump(s)
    last = len(hops)
    for n in range(N):
        HE[n] = HE[n] + PE[n] * KM[last, n : n + 1, :]

    def correct(j, _):
        r = pl.ds(pl.multiple_of(j * 8, 8), 8)
        reach, bc = SC[r, :], PR[r, R : R + 128]
        y = Y[r, :]
        for n in range(N):
            y = y + jnp.exp2(reach * slope[n]) * HE[n] * bc[:, N + n : N + n + 1]
        Y[r, :] = (y + d_skip[:, lane_c] * XA[r, :]) * ZS[r, :]
        return 0

    lax.fori_loop(0, J, correct, 0)
    back = (col == lax.rem(row, J) * 8 + lax.div(row, J)).astype(F32).astype(BF16)
    G[...] = dot(back, Y[...].astype(BF16)).astype(BF16)

    def swap(k):
        return remote(XS.at[k], XR.at[k], swap_s.at[k], swap_r.at[k], partner)

    def multiply(k):
        w = WO[emod(e + k)]
        XS[k] = dot(G[span(o, TL), :], w).astype(BF16)
        swap(k).start()
        MO[k] = dot(G[span(c, TL), :], w)

    each(0, NE, multiply)

    def out_send(k):
        return remote(OS.at[k], RO.at[k], out_s.at[k], out_r.at[k], at(emod(e + k), z, c))

    def reduce(k):
        swap(k).wait_recv()
        OS[k] = (MO[k] + XR[k].astype(F32)).astype(BF16)

    def reduce_send(k):
        reduce(k)
        out_send(k).start()

    each(1, NE, reduce_send)
    reduce(0)
    result = OS[0].astype(F32)
    for k in range(1, NE):
        out_send(k).wait_recv()
        result += RO[k].astype(F32)
    out[...] = result.astype(BF16)

    for copy in pairs:
        copy.wait_send()
    halo.wait_send()
    half.wait_send()
    rest.wait_send()
    for i in range(len(hops)):
        state_send(i).wait_send()

    def drain(k):
        tok_send(k).wait_send()
        sum_send(k).wait_send()
        all_send(k).wait_send()
        out_send(k).wait_send()

    each(1, NE, drain)

    def drain_pair(k):
        tok_fwd(k).wait_send()
        swap(k).wait_send()

    each(0, NE, drain_pair)

    def drain_ring(s):
        for p in range(3):
            for d in range(2):
                hop(p, d, s).wait_send()

    each(1, H, drain_ring)
    hop(0, 0, H).wait_send()
    hop(1, 1, H).wait_send()
    hop(2, 0, H).wait_send()


def local(
    tokens, segment_ids, w_in_x, w_in_z, conv_weight, conv_bias, w_xproj, w_dt, dt_bias,
    a_rate, d_skip, w_out,
):
    NE, NZ = lax.axis_size("expert"), lax.axis_size("fsdp") // 2
    TL, DC = tokens.shape
    KR_, C2 = w_in_x.shape
    CH, OC, R, N = C2 // 2, w_out.shape[1], w_dt.shape[0], a_rate.shape[1]
    T, J, H = 2 * TL, TL // 4, NZ // 2
    PW = R + 128
    z = lax.axis_index("fsdp") // 2
    padded = jnp.concatenate([jnp.full((3,), -1, jnp.int32), segment_ids], 0)
    window = lax.dynamic_slice_in_dim(padded, z * T, T + 3)
    same = jnp.stack([window[3 - k : 3 - k + T] == window[3:] for k in (1, 2, 3)])
    masks = same.reshape(3, 8, J).transpose(2, 1, 0).reshape(T, 3).astype(F32)
    masks = jnp.pad(masks, ((0, 0), (0, 125)))
    wxp = jnp.pad(w_xproj, ((0, 0), (0, PW - w_xproj.shape[1])))
    rounds = 2 + max(0, H.bit_length() - 2)
    sizes = (NE, NZ, TL, KR_, CH, OC, R, N)
    V = pltpu.VMEM
    dma = pltpu.SemaphoreType.DMA
    any_space = pl.BlockSpec(memory_space=pl.ANY)
    vmem = pl.BlockSpec(memory_space=pltpu.VMEM)
    return pl.pallas_call(
        functools.partial(kernel, sizes),
        out_shape=jax.ShapeDtypeStruct((TL, DC), BF16),
        in_specs=[any_space] * 4 + [vmem] * 8,
        out_specs=vmem,
        scratch_shapes=[
            V((NE, T, DC), BF16),
            V((NZ, 2 * KR_, CH), BF16),
            V((NZ, 2 * KR_, CH), BF16),
            V((NZ, CH, 2 * OC), BF16),
            V((T, CH), F32),
            V((T, CH), F32),
            V((T, CH), F32),
            V((24, CH), F32),
            V((T, CH), F32),
            V((T, CH), F32),
            V((T, PW), F32),
            V((TL, PW), F32),
            V((TL, PW), F32),
            V((NE, 8, PW), F32),
            V((T, PW), F32),
            V((T, CH), F32),
            V((T, CH), F32),
            V((T, CH), F32),
            V((T, CH), F32),
            V((N, 8, CH), F32),
            V((N, 8, CH), F32),
            V((rounds + 1, N + 8, CH), F32),
            V((rounds, N + 8, CH), F32),
            V((T, CH), BF16),
            V((NE, TL, DC), BF16),
            V((NE, TL, DC), BF16),
            V((NE, TL, DC), F32),
            V((NE, TL, DC), BF16),
            V((NE, TL, DC), BF16),
            dma((4,)),
            dma((3,)), dma((3,)),
            dma((NE,)), dma((NE,)),
            dma((NE,)), dma((NE,)),
            dma((3, 2, H + 1)), dma((3, 2, H + 1)),
            dma(()), dma(()),
            dma((2,)), dma((2,)),
            dma((NE,)), dma((NE,)),
            dma((NE,)), dma((NE,)),
            dma((rounds,)), dma((rounds,)),
            dma((NE,)), dma((NE,)),
            dma((NE,)), dma((NE,)),
        ],
        compiler_params=pltpu.CompilerParams(
            collective_id=0, has_side_effects=True, vmem_limit_bytes=48 * 1024 * 1024
        ),
    )(
        tokens, w_in_x, w_in_z, w_out, conv_weight, conv_bias[None, :], wxp, w_dt,
        dt_bias[None, :], a_rate.T, d_skip[None, :], masks,
    )


def solution(mesh):
    placed = (
        P("fsdp", "expert"),
        P(),
        P("fsdp", "expert"),
        P("fsdp", "expert"),
        P(None, "expert"),
        P("expert"),
        P("expert", None),
        P(None, "expert"),
        P("expert"),
        P("expert", None),
        P("expert"),
        P("expert", "fsdp"),
    )
    return jax.shard_map(
        local, mesh=mesh, in_specs=placed, out_specs=P("fsdp", "expert"), check_vma=False
    )
```

time: 576 us -> 137 us (0.24)
  waiting for transfers between devices: 332 us -> 0 us
  Pallas kernels: 0 us -> 133 us
  other arithmetic: 131 us -> 0.1 us
  blocking collectives: 64.4 us -> 0 us
  between operations: 13.7 us -> 0.2 us
  local copies, waits for them, and re-layouts: 16.4 us -> 3.57 us
  matrix products: 11.2 us -> 0 us
    all_gather x4 -> x0, waiting for transfers between devices: 140 us -> none  [the longest x1 77.2 us: local(): x_sum = add_rows(lax.all_gather(w_in_x, 'fsdp', axis=0, tiled=True))]
    pallas_call x0 -> x1, Pallas kernels: none -> 133 us  [local(): pl.pallas_call(functools.partial(kernel, sizes), out_shape=jax.ShapeDtype...]
    reduce_sum x49 -> x0, other arithmetic: 128 us -> none  [the longest x48 127 us: scan_step(): return (hidden_state, jnp.sum(hidden_state * c_t[None, :], axis=1))]
    psum x1 -> x0, waiting for transfers between devices: 107 us -> none  [local(): lax.psum(partial_proj.astype(jnp.bfloat16), 'expert').astype(jnp.float32)]
    reduce_scatter x1 -> x0, waiting for transfers between devices: 82.9 us -> none  [local(): lax.psum_scatter(partials.astype(jnp.bfloat16), 'expert', scatter_dimensi...]
    all_gather x2 -> x0, blocking collectives: 64.4 us -> none  [entering(): lax.all_gather(a.astype(kind), axis)]
    slice x23 -> x0, local copies, waits for them, and re-layouts: 14 us -> none  [the longest x16 10.9 us: local(): lax.scan(scan_step, zero_state, (delta, x_float, b_in, c_out, keep_mask),...]
    dot_general x4 -> x0, matrix products: 11.2 us -> none  [the longest x1 5.97 us: local(): jnp.dot(gated, lax.all_gather(w_out, 'fsdp', axis=1, tiled=True), preferr...]
  transfers between devices with their start and end apart: 7 -> 0, of which waited for: 4 -> 0; matrix products, arithmetic and copies ran while one was open for 26% -> 0% of each run, Pallas kernels for 0% -> 0%
where the time goes in v1:
time: 137 us
  Pallas kernels  133 us (97%)
  local copies, waits for them, and re-layouts  3.57 us (3%)
    pallas_call x1, Pallas kernels, local(): pl.pallas_call(functools.partial(kernel, sizes), out_shape=jax.ShapeDtype...  133 us
    unnamed x24, local copies, waits for them, and re-layouts  3.02 us

profile of v1, /device:TPU:1, one launch (start us, length us, event | category | flops | bytes accessed | tf_op | source)
XLA Modules:
  0.0 137.0 jit_solution(7672909806426759392)
XLA Ops:
  0.0 1.2 copy.14
  1.2 0.0 copy-start.10
  1.2 0.0 copy-start.1
  1.2 0.0 copy-start.2
  1.2 0.0 copy-start.3
  1.2 0.0 copy-start.4
  1.2 0.0 copy-start.5
  1.3 0.0 copy-start
  1.3 0.6 copy-done.10
  1.9 0.1 pad_dynamic-slice_fusion
  2.0 0.1 slice_compare_fusion.2
  2.1 0.1 eq.38
  2.1 0.1 eq.36
  2.2 0.1 eq.34
  2.3 0.2 copy.15
  2.5 0.0 copy-start.6
  2.5 0.0 copy-start.7
  2.5 0.0 copy-start.8
  2.5 0.0 copy-start.9
  2.6 0.0 copy-done.1
  2.6 0.0 copy-done.2
  2.6 0.0 copy-done.3
  2.6 0.0 copy-done.4
  2.6 0.0 copy-done.5
  2.6 0.0 copy-done
  2.6 0.6 copy-done.6
  3.2 0.0 copy-done.7
  3.2 0.0 copy-done.8
  3.2 0.0 copy-done.9
  3.2 133.2 %shard_map.118 = bf16[128,256]{1,0:T(8,128)(2,1)S(1)} custom-call(bf16[128,256]{1,0:T(8,128)(2,1)S(1)} %copy-done.4, bf16[128,512]{1,0:T(8,128)(2,1)S(1)} %copy-done.1, bf16[128,512]{1,0:T(8,128)(2,1)S(1)} %copy-done.2, bf16[512,128]{1,0:T(8,128)(2,1)S(1)} %copy-done.3, f32[4,512]{1,0:T(4,128)S(1)} %copy-done.6, f32[1,512]{1,0:T(1,128)S(1)} %bitcast.8, ...), custom_call_target="tpu_custom_call" | custom-call | tf_op jit(solution)/shard_map/pallas_call | solution.py:437
  136.4 0.6 copy.17
  (3 shorter events, 0.1 us)
Async XLA Ops:
  1.2 0.7 copy-start.10
  1.2 1.4 %copy-start.1 = (bf16[128,512]{1,0:T(8,128)(2,1)S(1)}, bf16[128,512]{1,0:T(8,128)(2,1)}, u32[]{:S(2)}) copy-start(bf16[128,512]{1,0:T(8,128)(2,1)} %wx.1) | copy-start | bytes 393220
  1.2 1.4 %copy-start.2 = (bf16[128,512]{1,0:T(8,128)(2,1)S(1)}, bf16[128,512]{1,0:T(8,128)(2,1)}, u32[]{:S(2)}) copy-start(bf16[128,512]{1,0:T(8,128)(2,1)} %wz.1) | copy-start | bytes 393220
  1.2 1.4 %copy-start.3 = (bf16[512,128]{1,0:T(8,128)(2,1)S(1)}, bf16[512,128]{1,0:T(8,128)(2,1)}, u32[]{:S(2)}) copy-start(bf16[512,128]{1,0:T(8,128)(2,1)} %wo.1) | copy-start | bytes 393220
  1.2 1.4 %copy-start.4 = (bf16[128,256]{1,0:T(8,128)(2,1)S(1)}, bf16[128,256]{1,0:T(8,128)(2,1)}, u32[]{:S(2)}) copy-start(bf16[128,256]{1,0:T(8,128)(2,1)} %tok.1) | copy-start | bytes 196612
  1.2 1.4 copy-start.5
  1.3 1.3 copy-start
  2.5 0.7 copy-start.6
  2.5 0.7 copy-start.7
  2.5 0.7 copy-start.8
  2.5 0.7 copy-start.9

commit v2 on v1

v2 whole, which is shorter than its diff:
```python
import functools
import math

import jax
import jax.numpy as jnp
from jax import lax
from jax.experimental import pallas as pl
from jax.experimental.pallas import tpu as pltpu
from jax.sharding import PartitionSpec as P

F32 = jnp.float32
BF16 = jnp.bfloat16
FAR = 1e30
LOG2E = 1.0 / math.log(2.0)
MESH = pl.DeviceIdType.MESH


def silu(v):
    return v * jax.nn.sigmoid(v)


def dot(a, b):
    return jnp.dot(a, b, preferred_element_type=F32)


def kernel(
    sizes,
    tok, wx, wz, wo, conv_w, conv_b, wxp, wdt, dt_bias, rates, d_skip, masks,
    out,
    TOK, WX, WZ, WO, AX, AZ, XP, HALO, XA, PB, RB, GB, PR,
    DD, DX, SC, Y, HE, PE, KM, KR, G, XS, XR, MO, OS, RO,
    local_sem, pair_s, pair_r, tok_s, tok_r, fwd_s, fwd_r, ring_s, ring_r,
    halo_s, halo_r, sum_s, sum_r, all_s, all_r,
    state_s, state_r, swap_s, swap_r, out_s, out_r,
):
    NE, NZ, TL, KR_, CH, OC, R, N = sizes
    T, J, H = 2 * TL, TL // 4, NZ // 2
    L = (R + 128) // 128
    CR = PB.shape[1]
    near = min(H, 4)
    far = [near * i for i in range(1, H // near)]
    e = lax.axis_index("expert")
    f = lax.axis_index("fsdp")
    z = lax.div(f, 2)
    c = lax.rem(f, 2)
    o = 1 - c

    def zmod(v):
        return lax.rem(v + 2 * NZ, NZ)

    def emod(v):
        return lax.rem(v + 2 * NE, NE)

    def at(e_, z_, c_):
        return (e_, 2 * z_ + c_)

    def remote(src, dst, ss, rs, dev):
        return pltpu.make_async_remote_copy(
            src_ref=src, dst_ref=dst, send_sem=ss, recv_sem=rs, device_id=dev, device_id_type=MESH
        )

    def span(i, n):
        return pl.ds(pl.multiple_of(i * n, n), n)

    def each(lo, hi, fn):
        def body(k, _):
            fn(k)
            return 0

        lax.fori_loop(lo, hi, body, 0)

    partner = at(e, z, o)

    own = [
        pltpu.make_async_copy(wx.at[:, span(c, CH)], WX.at[z, span(c, KR_)], local_sem.at[0]),
        pltpu.make_async_copy(wz.at[:, span(c, CH)], WZ.at[z, span(c, KR_)], local_sem.at[1]),
        pltpu.make_async_copy(wo.at[span(c, CH)], WO.at[z, :, span(c, OC)], local_sem.at[2]),
        pltpu.make_async_copy(tok, TOK.at[e, span(c, TL)], local_sem.at[3]),
    ]
    for copy in own:
        copy.start()

    barrier = pltpu.get_barrier_semaphore()

    def greet(dev):
        pl.semaphore_signal(barrier, inc=1, device_id=dev, device_id_type=MESH)

    friends = [partner]
    for d in sorted(set(range(1, near + 1)) | set(far)):
        friends += [at(e, zmod(z + d), c), at(e, zmod(z - d), c)]
    count = 1 + 2 * len(set(range(1, near + 1)) | set(far))
    if near == H and NZ == 2 * H and H < 3:
        friends = friends[:-1]
        count -= 1
    for dev in friends:
        greet(dev)

    def greet_plane(k):
        greet(at(emod(e + k), z, c))
        greet(at(emod(e + k), z, o))

    each(1, NE, greet_plane)
    pl.semaphore_wait(barrier, count + 2 * (NE - 1))

    def pair(p, side):
        src = [wx.at[:, span(o, CH)], wz.at[:, span(o, CH)], wo.at[span(o, CH)]][p]
        dst = [WX.at[z, span(side, KR_)], WZ.at[z, span(side, KR_)], WO.at[z, :, span(side, OC)]][p]
        return remote(src, dst, pair_s.at[p], pair_r.at[p], partner)

    pair(0, c).start()

    stacks = [WX, WZ, WO]

    def piece(p, block, h):
        rows = stacks[p].shape[1] // 2
        return stacks[p].at[block, span(h, rows)]

    def hop(p, d, s, h):
        sign = 1 - 2 * d
        block = zmod(z - sign * (s - 1))
        return remote(
            piece(p, block, h), piece(p, block, h),
            ring_s.at[p, d, s, h], ring_r.at[p, d, s, h], at(e, zmod(z + sign), c),
        )

    def arrive(p, d, s, h):
        sign = 1 - 2 * d
        block = zmod(z - sign * s)
        remote(
            piece(p, block, h), piece(p, block, h),
            ring_s.at[p, d, s, h], ring_r.at[p, d, s, h], at(e, zmod(z + sign), c),
        ).wait_recv()

    own[0].wait()
    hop(0, 0, 1, c).start()
    hop(0, 1, 1, c).start()
    pair(1, c).start()
    pair(2, c).start()

    def tok_send(k):
        return remote(
            tok, TOK.at[e, span(c, TL)], tok_s.at[k], tok_r.at[k], at(emod(e + k), z, c)
        )

    def tok_in(k):
        return remote(
            tok, TOK.at[emod(e - k), span(c, TL)], tok_s.at[k], tok_r.at[k], partner
        )

    def tok_fwd(k):
        b = emod(e - k)
        return remote(
            TOK.at[b, span(c, TL)], TOK.at[b, span(c, TL)], fwd_s.at[k], fwd_r.at[k], partner
        )

    def tok_fwd_in(k):
        b = emod(e - k)
        return remote(
            TOK.at[b, span(o, TL)], TOK.at[b, span(o, TL)], fwd_s.at[k], fwd_r.at[k], partner
        )

    pair(0, o).wait_recv()
    hop(0, 0, 1, o).start()
    hop(0, 1, 1, o).start()
    each(1, NE, lambda k: tok_send(k).start())
    own[3].wait()
    tok_fwd(0).start()

    def begin(p):
        own[p].wait()
        pair(p, o).wait_recv()
        for h in (0, 1):
            for d in (0, 1):
                hop(p, d, 1, h).start()

    def step(p, s):
        for h in (0, 1):
            for d in (0, 1):
                if s < H or d == h:
                    arrive(p, d, s, h)
                    if s < H - 1 or (s == H - 1 and d == h):
                        hop(p, d, s + 1, h).start()

    def add(acc, w, block, first=False):
        product = dot(TOK[block], w[block])
        acc[...] = product if first else acc[...] + product

    def add_step(acc, w, s):
        add(acc, w, zmod(z - s))
        if s < H:
            add(acc, w, zmod(z + s))

    done = 0
    for s in range(1, H + 1):
        step(0, s)
        if s == H - 1:
            begin(1)
        if s == 1:

            def relay(k):
                tok_in(k).wait_recv()
                tok_fwd(k).start()

            each(1, NE, relay)
        if s == min(3, H):
            each(0, NE, lambda k: tok_fwd_in(k).wait_recv())
            add(AX, WX, z, first=True)
        if s > 3:
            for s_ in range(done + 1, s - 1):
                add_step(AX, WX, s_)
            done = max(done, s - 2)
    for s in range(done + 1, H + 1):
        add_step(AX, WX, s)

    events = [(1, s) for s in range(1, H + 1)] + [(2, s) for s in range(1, H + 1)]
    position = [0]

    def pump(upto):
        while position[0] < min(upto, len(events)):
            p, s = events[position[0]]
            position[0] += 1
            step(p, s)
            if p == 1:
                if s == H - 1:
                    begin(2)
                if s == 1:
                    add(AZ, WZ, z, first=True)
                add_step(AZ, WZ, s)

    row = lax.broadcasted_iota(jnp.int32, (T, T), 0)
    col = lax.broadcasted_iota(jnp.int32, (T, T), 1)
    perm = (col == lax.rem(row, 8) * J + lax.div(row, 8)).astype(F32).astype(BF16)
    XP[...] = dot(perm, AX[...].astype(BF16))
    rim = XP.at[pl.ds((J - 3) * 8, 24)]
    halo = remote(rim, HALO, halo_s, halo_r, at(e, zmod(z + 1), c))
    halo.start()
    pump(1)
    halo.wait_recv()
    lane_c = span(c, CH)
    top = lax.broadcasted_iota(jnp.int32, (8, CH), 0) == 0
    early = []
    for i in range(3):
        mine = pltpu.roll(XP[(J - 3 + i) * 8 : (J - 2 + i) * 8], 1, 0)
        theirs = pltpu.roll(HALO[i * 8 : (i + 1) * 8], 1, 0)
        early.append(jnp.where(top, theirs, mine))
    ext = jnp.concatenate(early + [XP[...]], 0)
    conv = conv_b[:, lane_c] + conv_w[3:4, lane_c] * ext[24:]
    for k in range(1, 4):
        conv += conv_w[3 - k : 4 - k, lane_c] * ext[24 - 8 * k : 24 - 8 * k + T] * masks[:, k - 1 : k]
    x_act = silu(conv).astype(BF16)
    XA[...] = x_act.astype(F32)
    PR[...] = dot(x_act, wxp[span(c, CH), :])

    blank = [jnp.zeros((CR - 8 * L, 128), F32)] if CR > 8 * L else []

    def pack(q):
        rows = span(q, 8)
        tiles = [PR[rows, l * 128 : (l + 1) * 128] for l in range(L)]
        PB[q] = jnp.concatenate(tiles + blank, 0).astype(BF16)

    each(0, 2 * NE, pack)

    def plane(k, rel):
        core = c if rel == 0 else o
        return emod(e + k), core

    def sum_send(k, rel):
        e_, core = plane(k, rel)
        return remote(
            PB.at[core * NE + e_], RB.at[rel * NE + k],
            sum_s.at[rel, k], sum_r.at[rel, k], at(e_, z, core),
        )

    mine = c * NE + e

    def all_send(k, rel):
        e_, core = plane(k, rel)
        return remote(
            GB.at[mine], GB.at[mine], all_s.at[rel, k], all_r.at[rel, k], at(e_, z, core)
        )

    def all_in(k, rel):
        e_, core = plane(-k, rel)
        theirs = core * NE + e_
        return remote(
            GB.at[theirs], GB.at[theirs], all_s.at[rel, k], all_r.at[rel, k], at(e_, z, core)
        )

    def everyone(fn):
        fn(0, 1)

        def both(k):
            fn(k, 1)
            fn(k, 0)

        each(1, NE, both)

    everyone(lambda k, rel: sum_send(k, rel).start())
    pump(3)
    everyone(lambda k, rel: sum_send(k, rel).wait_recv())
    total = PB[mine].astype(F32)
    for k in range(1, 2 * NE):
        total += RB[k].astype(F32)
    GB[mine] = total.astype(BF16)
    everyone(lambda k, rel: all_send(k, rel).start())
    pump(4)
    everyone(lambda k, rel: all_in(k, rel).wait_recv())

    def unpack(q):
        chunk = GB[q].astype(F32)
        for l in range(L):
            PR[span(q, 8), l * 128 : (l + 1) * 128] = chunk[8 * l : 8 * l + 8]

    each(0, 2 * NE, unpack)
    pump(5)
    delta = dot(PR[:, :R].astype(BF16), wdt[:, lane_c]) + dt_bias[:, lane_c]
    delta = jnp.maximum(delta, 0.0) + jnp.log1p(jnp.exp(-jnp.abs(delta)))
    DX[...] = delta * XA[...]
    DD[...] = delta + (1.0 - masks[:, 0:1]) * FAR

    slope = [rates[n : n + 1, lane_c] * (-LOG2E) for n in range(N)]

    def forward(j, carry):
        hs, reach = carry
        r = pl.ds(pl.multiple_of(j * 8, 8), 8)
        dd, dx, bc = DD[r, :], DX[r, :], PR[r, R : R + 128]
        reach = reach + dd
        SC[r, :] = reach
        y = jnp.zeros((8, CH), F32)
        later = []
        for n in range(N):
            h = jnp.exp2(dd * slope[n]) * hs[n] + dx * bc[:, n : n + 1]
            y = y + h * bc[:, N + n : N + n + 1]
            later.append(h)
        Y[r, :] = y
        return later, reach

    zero = jnp.zeros((8, CH), F32)
    middle = lax.fori_loop(0, J // 2, forward, ([zero] * N, zero))
    pump(6)
    ends, reach = lax.fori_loop(J // 2, J, forward, middle)
    sub = lax.broadcasted_iota(jnp.int32, (8, CH), 0)
    states = []
    for n in range(N):
        h, p = ends[n], jnp.exp2(reach * slope[n])
        for d in (1, 2, 4):
            before = sub >= d
            h = h + p * jnp.where(before, pltpu.roll(h, d, 0), 0.0)
            p = p * jnp.where(before, pltpu.roll(p, d, 0), 1.0)
        HE[n] = jnp.where(top, 0.0, pltpu.roll(h, 1, 0))
        PE[n] = jnp.where(top, 1.0, pltpu.roll(p, 1, 0))
        states.append(h[7:8])
    span_sum = jnp.broadcast_to(jnp.sum(reach, axis=0, keepdims=True), (N, CH))
    KM[0] = jnp.concatenate(states + [span_sum], 0).astype(BF16)

    steep = rates[:, lane_c] * (-LOG2E)

    def state_send(i):
        d = i + 1 if i < near else far[i - near]
        return remote(
            KM.at[0 if i < near else 1], KR.at[i], state_s.at[i], state_r.at[i],
            at(e, zmod(z + d), c),
        )

    def join(earlier, latter):
        both = latter.astype(F32)
        h, reach = both[:N], both[N:]
        if earlier is None:
            return h, reach
        return jnp.exp2(reach * steep) * earlier[0] + h, earlier[1] + reach

    for i in range(near):
        state_send(i).start()
    pump(8)
    for i in range(near):
        state_send(i).wait_recv()
    entering = None
    for i in range(near - 1, -1, -1):
        entering = join(entering, KR[i])
    if far:
        KM[1] = jnp.concatenate(entering, 0).astype(BF16)
        for i in range(near, near + len(far)):
            state_send(i).start()
        pump(9)
        for i in range(near, near + len(far)):
            state_send(i).wait_recv()
        combined = None
        for i in range(near + len(far) - 1, near - 1, -1):
            combined = join(combined, KR[i])
        entering = join(combined, KM[1])
    pump(10)
    for n in range(N):
        HE[n] = HE[n] + PE[n] * entering[0][n : n + 1, :]

    AZ[...] = silu(dot(perm, AZ[...].astype(BF16)))

    def correct(j, _):
        r = pl.ds(pl.multiple_of(j * 8, 8), 8)
        reach, bc = SC[r, :], PR[r, R : R + 128]
        y = Y[r, :]
        for n in range(N):
            y = y + jnp.exp2(reach * slope[n]) * HE[n] * bc[:, N + n : N + n + 1]
        Y[r, :] = (y + d_skip[:, lane_c] * XA[r, :]) * AZ[r, :]
        return 0

    lax.fori_loop(0, J, correct, 0)
    back = (col == lax.rem(row, J) * 8 + lax.div(row, J)).astype(F32).astype(BF16)
    G[...] = dot(back, Y[...].astype(BF16)).astype(BF16)

    def swap(k):
        return remote(XS.at[k], XR.at[k], swap_s.at[k], swap_r.at[k], partner)

    def out_send(k):
        return remote(OS.at[k], RO.at[k], out_s.at[k], out_r.at[k], at(emod(e + k), z, c))

    def group(low, high):
        total = 2 * (high - low + 1) - (low == 0) - (high == H)

        def offset(i):
            i = lax.rem(i + e, total)
            if low == 0:
                return lax.div(i + 1, 2) * (1 - 2 * lax.rem(i, 2))
            return (low + lax.div(i, 2)) * (1 - 2 * lax.rem(i, 2))

        def multiply(i):
            block = zmod(z + offset(i))
            k = emod(block - e)
            w = WO[block]
            XS[k] = dot(G[span(o, TL), :], w).astype(BF16)
            swap(k).start()
            MO[k] = dot(G[span(c, TL), :], w)

        each(0, total, multiply)

        def reduce(i):
            k = emod(zmod(z + offset(i)) - e)
            swap(k).wait_recv()
            both = (MO[k] + XR[k].astype(F32)).astype(BF16)
            OS[k] = both

            @pl.when(k > 0)
            def _():
                out_send(k).start()

        each(0, total, reduce)

    if H > 5:
        pump(H + 3)
        group(0, 3)
        pump(H + 5)
        group(4, 5)
        pump(2 * H)
        group(6, H)
    else:
        pump(2 * H)
        group(0, H)
    result = OS[0].astype(F32)
    for k in range(1, NE):
        out_send(k).wait_recv()
        result += RO[k].astype(F32)
    out[...] = result.astype(BF16)

    for p in range(3):
        pair(p, c).wait_send()
    halo.wait_send()
    for i in range(near + len(far)):
        state_send(i).wait_send()

    def drain(k):
        tok_send(k).wait_send()
        out_send(k).wait_send()

    each(1, NE, drain)

    def drain_all(k, rel):
        sum_send(k, rel).wait_send()
        all_send(k, rel).wait_send()

    everyone(drain_all)

    def drain_pair(k):
        tok_fwd(k).wait_send()
        swap(k).wait_send()

    each(0, NE, drain_pair)

    def drain_ring(s):
        for p in range(3):
            for d in range(2):
                for h in range(2):
                    hop(p, d, s, h).wait_send()

    each(1, H, drain_ring)
    for p in range(3):
        for h in range(2):
            hop(p, h, H, h).wait_send()


def local(
    tokens, segment_ids, w_in_x, w_in_z, conv_weight, conv_bias, w_xproj, w_dt, dt_bias,
    a_rate, d_skip, w_out,
):
    NE, NZ = lax.axis_size("expert"), lax.axis_size("fsdp") // 2
    TL, DC = tokens.shape
    KR_, C2 = w_in_x.shape
    CH, OC, R, N = C2 // 2, w_out.shape[1], w_dt.shape[0], a_rate.shape[1]
    T, J, H = 2 * TL, TL // 4, NZ // 2
    PW = R + 128
    z = lax.axis_index("fsdp") // 2
    padded = jnp.concatenate([jnp.full((3,), -1, jnp.int32), segment_ids], 0)
    window = lax.dynamic_slice_in_dim(padded, z * T, T + 3)
    same = jnp.stack([window[3 - k : 3 - k + T] == window[3:] for k in (1, 2, 3)])
    masks = same.reshape(3, 8, J).transpose(2, 1, 0).reshape(T, 3).astype(F32)
    masks = jnp.pad(masks, ((0, 0), (0, 125)))
    wxp = jnp.pad(w_xproj, ((0, 0), (0, PW - w_xproj.shape[1])))
    near = min(H, 4)
    rounds = near + H // near - 1
    CR = -(-PW // 256) * 16
    sizes = (NE, NZ, TL, KR_, CH, OC, R, N)
    V = pltpu.VMEM
    dma = pltpu.SemaphoreType.DMA
    any_space = pl.BlockSpec(memory_space=pl.ANY)
    vmem = pl.BlockSpec(memory_space=pltpu.VMEM)
    return pl.pallas_call(
        functools.partial(kernel, sizes),
        out_shape=jax.ShapeDtypeStruct((TL, DC), BF16),
        in_specs=[any_space] * 4 + [vmem] * 8,
        out_specs=vmem,
        scratch_shapes=[
            V((NE, T, DC), BF16),
            V((NZ, 2 * KR_, CH), BF16),
            V((NZ, 2 * KR_, CH), BF16),
            V((NZ, CH, 2 * OC), BF16),
            V((T, CH), F32),
            V((T, CH), F32),
            V((T, CH), F32),
            V((24, CH), F32),
            V((T, CH), F32),
            V((2 * NE, CR, 128), BF16),
            V((2 * NE, CR, 128), BF16),
            V((2 * NE, CR, 128), BF16),
            V((T, PW), F32),
            V((T, CH), F32),
            V((T, CH), F32),
            V((T, CH), F32),
            V((T, CH), F32),
            V((N, 8, CH), F32),
            V((N, 8, CH), F32),
            V((2, 2 * N, CH), BF16),
            V((rounds, 2 * N, CH), BF16),
            V((T, CH), BF16),
            V((NE, TL, DC), BF16),
            V((NE, TL, DC), BF16),
            V((NE, TL, DC), F32),
            V((NE, TL, DC), BF16),
            V((NE, TL, DC), BF16),
            dma((4,)),
            dma((3,)), dma((3,)),
            dma((NE,)), dma((NE,)),
            dma((NE,)), dma((NE,)),
            dma((3, 2, H + 1, 2)), dma((3, 2, H + 1, 2)),
            dma(()), dma(()),
            dma((2, NE)), dma((2, NE)),
            dma((2, NE)), dma((2, NE)),
            dma((rounds,)), dma((rounds,)),
            dma((NE,)), dma((NE,)),
            dma((NE,)), dma((NE,)),
        ],
        compiler_params=pltpu.CompilerParams(
            collective_id=0, has_side_effects=True, vmem_limit_bytes=48 * 1024 * 1024
        ),
    )(
        tokens, w_in_x, w_in_z, w_out, conv_weight, conv_bias[None, :], wxp, w_dt,
        dt_bias[None, :], a_rate.T, d_skip[None, :], masks,
    )


def solution(mesh):
    placed = (
        P("fsdp", "expert"),
        P(),
        P("fsdp", "expert"),
        P("fsdp", "expert"),
        P(None, "expert"),
        P("expert"),
        P("expert", None),
        P(None, "expert"),
        P("expert"),
        P("expert", None),
        P("expert"),
        P("expert", "fsdp"),
    )
    return jax.shard_map(
        local, mesh=mesh, in_specs=placed, out_specs=P("fsdp", "expert"), check_vma=False
    )
```

time: 137 us -> 149 us (1.088)
  the two profiles are of different devices: /device:TPU:1 before, /device:TPU:5 now
where the time goes in v2:
time: 149 us; the launch traced here: 148 us
  Pallas kernels  144 us (97%)
  local copies, waits for them, and re-layouts  3.57 us (2%)
    pallas_call x1, Pallas kernels, local(): pl.pallas_call(functools.partial(kernel, sizes), out_shape=jax.ShapeDtype...  144 us
    unnamed x24, local copies, waits for them, and re-layouts  3.02 us

profile of v2, /device:TPU:5, one launch (start us, length us, event | category | flops | bytes accessed | tf_op | source)
XLA Modules:
  0.0 148.3 jit_solution(6317372758171674428)
XLA Ops:
  0.0 1.2 copy.14
  1.2 0.0 copy-start.10
  1.2 0.0 copy-start.1
  1.2 0.0 copy-start.2
  1.2 0.0 copy-start.3
  1.2 0.0 copy-start.4
  1.2 0.0 copy-start.5
  1.3 0.0 copy-start
  1.3 0.6 copy-done.10
  1.9 0.1 pad_dynamic-slice_fusion
  2.0 0.1 slice_compare_fusion.2
  2.1 0.1 eq.38
  2.1 0.1 eq.36
  2.2 0.1 eq.34
  2.3 0.2 copy.15
  2.5 0.0 copy-start.6
  2.5 0.0 copy-start.7
  2.5 0.0 copy-start.8
  2.5 0.0 copy-start.9
  2.6 0.0 copy-done.1
  2.6 0.0 copy-done.2
  2.6 0.0 copy-done.3
  2.6 0.0 copy-done.4
  2.6 0.0 copy-done.5
  2.6 0.0 copy-done
  2.6 0.6 copy-done.6
  3.2 0.0 copy-done.7
  3.2 0.0 copy-done.8
  3.2 0.0 copy-done.9
  3.2 144.5 %shard_map.118 = bf16[128,256]{1,0:T(8,128)(2,1)S(1)} custom-call(bf16[128,256]{1,0:T(8,128)(2,1)S(1)} %copy-done.4, bf16[128,512]{1,0:T(8,128)(2,1)S(1)} %copy-done.1, bf16[128,512]{1,0:T(8,128)(2,1)S(1)} %copy-done.2, bf16[512,128]{1,0:T(8,128)(2,1)S(1)} %copy-done.3, f32[4,512]{1,0:T(4,128)S(1)} %copy-done.6, f32[1,512]{1,0:T(1,128)S(1)} %bitcast.8, ...), custom_call_target="tpu_custom_call" | custom-call | tf_op jit(solution)/shard_map/pallas_call | solution.py:524
  147.7 0.6 copy.17
  (3 shorter events, 0.1 us)
Async XLA Ops:
  1.2 0.7 copy-start.10
  1.2 1.4 copy-start.1
  1.2 1.4 copy-start.2
  1.2 1.4 copy-start.3
  1.2 1.4 copy-start.4
  1.2 1.4 copy-start.5
  1.3 1.3 copy-start
  2.5 0.7 copy-start.6
  2.5 0.7 copy-start.7
  2.5 0.7 copy-start.8
  2.5 0.7 copy-start.9

commit v3 on v2

--- a/solution.py
+++ b/solution.py
@@ -190,42 +190,48 @@
         if s < H:
             add(acc, w, zmod(z + s))
 
+    def relay(k):
+        tok_in(k).wait_recv()
+        tok_fwd(k).start()
+
+    relay_at, tokens_at = min(4, H - 1), min(7, H)
+    z_after = {2 * i + 1: i for i in range(1, H) if 2 * i + 1 < H}
+    z_done = len(z_after)
     done = 0
     for s in range(1, H + 1):
         step(0, s)
+        if s == 1:
+            begin(1)
+        if s in z_after:
+            step(1, z_after[s])
         if s == H - 1:
-            begin(1)
-        if s == 1:
-
-            def relay(k):
-                tok_in(k).wait_recv()
-                tok_fwd(k).start()
-
+            begin(2)
+        if s == relay_at:
             each(1, NE, relay)
-        if s == min(3, H):
+        if s == tokens_at:
             each(0, NE, lambda k: tok_fwd_in(k).wait_recv())
             add(AX, WX, z, first=True)
-        if s > 3:
-            for s_ in range(done + 1, s - 1):
+        if s >= tokens_at:
+            for s_ in range(done + 1, s):
                 add_step(AX, WX, s_)
-            done = max(done, s - 2)
-    for s in range(done + 1, H + 1):
-        add_step(AX, WX, s)
-
-    events = [(1, s) for s in range(1, H + 1)] + [(2, s) for s in range(1, H + 1)]
+            done = s - 1
+    add_step(AX, WX, H)
+
     position = [0]
 
     def pump(upto):
-        while position[0] < min(upto, len(events)):
-            p, s = events[position[0]]
+        while position[0] < min(upto, H):
             position[0] += 1
-            step(p, s)
-            if p == 1:
-                if s == H - 1:
-                    begin(2)
-                if s == 1:
-                    add(AZ, WZ, z, first=True)
-                add_step(AZ, WZ, s)
+            s = position[0]
+            if s + z_done <= H:
+                step(1, s + z_done)
+            step(2, s)
+            if s == 1:
+                add(AZ, WZ, z, first=True)
+                for i in range(1, z_done + 1):
+                    add_step(AZ, WZ, i)
+            if s + z_done <= H:
+                add_step(AZ, WZ, s + z_done)
 
     row = lax.broadcasted_iota(jnp.int32, (T, T), 0)
     col = lax.broadcasted_iota(jnp.int32, (T, T), 1)
@@ -234,7 +240,6 @@
     rim = XP.at[pl.ds((J - 3) * 8, 24)]
     halo = remote(rim, HALO, halo_s, halo_r, at(e, zmod(z + 1), c))
     halo.start()
-    pump(1)
     halo.wait_recv()
     lane_c = span(c, CH)
     top = lax.broadcasted_iota(jnp.int32, (8, CH), 0) == 0
@@ -251,6 +256,7 @@
     XA[...] = x_act.astype(F32)
     PR[...] = dot(x_act, wxp[span(c, CH), :])
 
+    pump(1)
     blank = [jnp.zeros((CR - 8 * L, 128), F32)] if CR > 8 * L else []
 
     def pack(q):
@@ -296,14 +302,14 @@
         each(1, NE, both)
 
     everyone(lambda k, rel: sum_send(k, rel).start())
-    pump(3)
+    pump(2)
     everyone(lambda k, rel: sum_send(k, rel).wait_recv())
     total = PB[mine].astype(F32)
     for k in range(1, 2 * NE):
         total += RB[k].astype(F32)
     GB[mine] = total.astype(BF16)
     everyone(lambda k, rel: all_send(k, rel).start())
-    pump(4)
+    pump(3)
     everyone(lambda k, rel: all_in(k, rel).wait_recv())
 
     def unpack(q):
@@ -312,7 +318,7 @@
             PR[span(q, 8), l * 128 : (l + 1) * 128] = chunk[8 * l : 8 * l + 8]
 
     each(0, 2 * NE, unpack)
-    pump(5)
+    pump(4)
     delta = dot(PR[:, :R].astype(BF16), wdt[:, lane_c]) + dt_bias[:, lane_c]
     delta = jnp.maximum(delta, 0.0) + jnp.log1p(jnp.exp(-jnp.abs(delta)))
     DX[...] = delta * XA[...]
@@ -336,9 +342,7 @@
         return later, reach
 
     zero = jnp.zeros((8, CH), F32)
-    middle = lax.fori_loop(0, J // 2, forward, ([zero] * N, zero))
-    pump(6)
-    ends, reach = lax.fori_loop(J // 2, J, forward, middle)
+    ends, reach = lax.fori_loop(0, J, forward, ([zero] * N, zero))
     sub = lax.broadcasted_iota(jnp.int32, (8, CH), 0)
     states = []
     for n in range(N):
@@ -371,7 +375,7 @@
 
     for i in range(near):
         state_send(i).start()
-    pump(8)
+    pump(5)
     for i in range(near):
         state_send(i).wait_recv()
     entering = None
@@ -381,18 +385,16 @@
         KM[1] = jnp.concatenate(entering, 0).astype(BF16)
         for i in range(near, near + len(far)):
             state_send(i).start()
-        pump(9)
+        pump(6)
         for i in range(near, near + len(far)):
             state_send(i).wait_recv()
         combined = None
         for i in range(near + len(far) - 1, near - 1, -1):
             combined = join(combined, KR[i])
         entering = join(combined, KM[1])
-    pump(10)
+    pump(7)
     for n in range(N):
         HE[n] = HE[n] + PE[n] * entering[0][n : n + 1, :]
-
-    AZ[...] = silu(dot(perm, AZ[...].astype(BF16)))
 
     def correct(j, _):
         r = pl.ds(pl.multiple_of(j * 8, 8), 8)
@@ -400,12 +402,14 @@
         y = Y[r, :]
         for n in range(N):
             y = y + jnp.exp2(reach * slope[n]) * HE[n] * bc[:, N + n : N + n + 1]
-        Y[r, :] = (y + d_skip[:, lane_c] * XA[r, :]) * AZ[r, :]
+        Y[r, :] = y + d_skip[:, lane_c] * XA[r, :]
         return 0
 
     lax.fori_loop(0, J, correct, 0)
     back = (col == lax.rem(row, J) * 8 + lax.div(row, J)).astype(F32).astype(BF16)
-    G[...] = dot(back, Y[...].astype(BF16)).astype(BF16)
+    pump(H)
+    gate = silu(dot(perm, AZ[...].astype(BF16)))
+    G[...] = dot(back, (Y[...] * gate).astype(BF16)).astype(BF16)
 
     def swap(k):
         return remote(XS.at[k], XR.at[k], swap_s.at[k], swap_r.at[k], partner)
@@ -430,30 +434,26 @@
             swap(k).start()
             MO[k] = dot(G[span(c, TL), :], w)
 
-        each(0, total, multiply)
-
         def reduce(i):
             k = emod(zmod(z + offset(i)) - e)
             swap(k).wait_recv()
-            both = (MO[k] + XR[k].astype(F32)).astype(BF16)
-            OS[k] = both
+            OS[k] = (MO[k] + XR[k].astype(F32)).astype(BF16)
 
             @pl.when(k > 0)
             def _():
                 out_send(k).start()
 
-        each(0, total, reduce)
-
-    if H > 5:
-        pump(H + 3)
-        group(0, 3)
-        pump(H + 5)
-        group(4, 5)
-        pump(2 * H)
-        group(6, H)
-    else:
-        pump(2 * H)
-        group(0, H)
+        ahead = min(3, total)
+        each(0, ahead, multiply)
+
+        def both(i):
+            multiply(i)
+            reduce(i - ahead)
+
+        each(ahead, total, both)
+        each(total - ahead, total, reduce)
+
+    group(0, H)
     result = OS[0].astype(F32)
     for k in range(1, NE):
         out_send(k).wait_recv()

time: 149 us -> 125 us (0.84)
  the two profiles are of different devices: /device:TPU:5 before, /device:TPU:1 now
where the time goes in v3:
time: 125 us
  Pallas kernels  121 us (97%)
  local copies, waits for them, and re-layouts  3.57 us (3%)
    pallas_call x1, Pallas kernels, local(): pl.pallas_call(functools.partial(kernel, sizes), out_shape=jax.ShapeDtype...  121 us
    unnamed x24, local copies, waits for them, and re-layouts  3.02 us

profile of v3, /device:TPU:1, one launch (start us, length us, event | category | flops | bytes accessed | tf_op | source)
XLA Modules:
  0.0 124.6 jit_solution(5464052819280438628)
XLA Ops:
  0.0 1.2 copy.14
  1.2 0.0 copy-start.10
  1.2 0.0 copy-start.1
  1.2 0.0 copy-start.2
  1.2 0.0 copy-start.3
  1.2 0.0 copy-start.4
  1.2 0.0 copy-start.5
  1.3 0.0 copy-start
  1.3 0.6 copy-done.10
  1.9 0.1 pad_dynamic-slice_fusion
  2.0 0.1 slice_compare_fusion.2
  2.1 0.1 eq.38
  2.1 0.1 eq.36
  2.2 0.1 eq.34
  2.3 0.2 copy.15
  2.5 0.0 copy-start.6
  2.5 0.0 copy-start.7
  2.5 0.0 copy-start.8
  2.5 0.0 copy-start.9
  2.6 0.0 copy-done.1
  2.6 0.0 copy-done.2
  2.6 0.0 copy-done.3
  2.6 0.0 copy-done.4
  2.6 0.0 copy-done.5
  2.6 0.0 copy-done
  2.6 0.6 copy-done.6
  3.2 0.0 copy-done.7
  3.2 0.0 copy-done.8
  3.2 0.0 copy-done.9
  3.2 120.7 %shard_map.118 = bf16[128,256]{1,0:T(8,128)(2,1)S(1)} custom-call(bf16[128,256]{1,0:T(8,128)(2,1)S(1)} %copy-done.4, bf16[128,512]{1,0:T(8,128)(2,1)S(1)} %copy-done.1, bf16[128,512]{1,0:T(8,128)(2,1)S(1)} %copy-done.2, bf16[512,128]{1,0:T(8,128)(2,1)S(1)} %copy-done.3, f32[4,512]{1,0:T(4,128)S(1)} %copy-done.6, f32[1,512]{1,0:T(1,128)S(1)} %bitcast.8, ...), custom_call_target="tpu_custom_call" | custom-call | tf_op jit(solution)/shard_map/pallas_call | solution.py:524
  124.0 0.6 copy.17
  (3 shorter events, 0.1 us)
Async XLA Ops:
  1.2 0.7 copy-start.10
  1.2 1.4 %copy-start.1 = (bf16[128,512]{1,0:T(8,128)(2,1)S(1)}, bf16[128,512]{1,0:T(8,128)(2,1)}, u32[]{:S(2)}) copy-start(bf16[128,512]{1,0:T(8,128)(2,1)} %wx.1) | copy-start | bytes 393220
  1.2 1.4 %copy-start.2 = (bf16[128,512]{1,0:T(8,128)(2,1)S(1)}, bf16[128,512]{1,0:T(8,128)(2,1)}, u32[]{:S(2)}) copy-start(bf16[128,512]{1,0:T(8,128)(2,1)} %wz.1) | copy-start | bytes 393220
  1.2 1.4 %copy-start.3 = (bf16[512,128]{1,0:T(8,128)(2,1)S(1)}, bf16[512,128]{1,0:T(8,128)(2,1)}, u32[]{:S(2)}) copy-start(bf16[512,128]{1,0:T(8,128)(2,1)} %wo.1) | copy-start | bytes 393220
  1.2 1.4 %copy-start.4 = (bf16[128,256]{1,0:T(8,128)(2,1)S(1)}, bf16[128,256]{1,0:T(8,128)(2,1)}, u32[]{:S(2)}) copy-start(bf16[128,256]{1,0:T(8,128)(2,1)} %tok.1) | copy-start | bytes 196612
  1.2 1.4 %copy-start.5 = (f32[512,16]{0,1:T(8,128)S(1)}, f32[512,16]{0,1:T(8,128)}, u32[]{:S(2)}) copy-start(f32[512,16]{0,1:T(8,128)} %param.21) | copy-start | bytes 98308
  1.3 1.3 %copy-start = (bf16[256,512]{1,0:T(8,128)(2,1)S(1)}, bf16[256,512]{1,0:T(8,128)(2,1)}, u32[]{:S(2)}) copy-start(bf16[256,512]{1,0:T(8,128)(2,1)} %wdt.1) | copy-start | bytes 786436
  2.5 0.7 copy-start.6
  2.5 0.7 copy-start.7
  2.5 0.7 copy-start.8
  2.5 0.7 copy-start.9

commit v4 on v3

--- a/solution.py
+++ b/solution.py
@@ -25,13 +25,13 @@
 
 def kernel(
     sizes,
-    tok, wx, wz, wo, conv_w, conv_b, wxp, wdt, dt_bias, rates, d_skip, masks,
+    tok, wx, wz, wo, conv_w, conv_b, wxp, wdt, dt_bias, rates, d_skip, ids,
     out,
-    TOK, WX, WZ, WO, AX, AZ, XP, HALO, XA, PB, RB, GB, PR,
-    DD, DX, SC, Y, HE, PE, KM, KR, G, XS, XR, MO, OS, RO,
+    TOK, WX, WZ, WO, WP, AX, AZ, XP, HALO, XA, PB, RB, GB, PR,
+    DD, DX, SC, Y, HE, PE, KM, KR, KS, SR, MASK, PERM, G, GP, MO, OS, RO,
     local_sem, pair_s, pair_r, tok_s, tok_r, fwd_s, fwd_r, ring_s, ring_r,
     halo_s, halo_r, sum_s, sum_r, all_s, all_r,
-    state_s, state_r, swap_s, swap_r, out_s, out_r,
+    state_s, state_r, reach_s, reach_r, gate_s, gate_r, rest_s, rest_r, out_s, out_r,
 ):
     NE, NZ, TL, KR_, CH, OC, R, N = sizes
     T, J, H = 2 * TL, TL // 4, NZ // 2
@@ -80,6 +80,23 @@
     for copy in own:
         copy.start()
 
+    row = lax.broadcasted_iota(jnp.int32, (T, T), 0)
+    col = lax.broadcasted_iota(jnp.int32, (T, T), 1)
+    PERM[...] = (col == lax.rem(row, 8) * J + lax.div(row, 8)).astype(F32).astype(BF16)
+
+    here = jnp.broadcast_to(ids[pl.ds(z, 1), :], (8, T))
+    previous = jnp.broadcast_to(ids[pl.ds(zmod(z - 1), 1), :], (8, T))
+    lane = lax.broadcasted_iota(jnp.int32, (8, T), 1)
+    line = lax.broadcasted_iota(jnp.int32, (8, T), 0)
+    same = jnp.zeros((8, T), F32)
+    for k in range(1, 4):
+        shifted = jnp.where(lane >= k, pltpu.roll(here, k, 1), pltpu.roll(previous, k, 1))
+        inside = lane + z * T >= k
+        same = jnp.where((line == k - 1) & inside & (shifted == here), 1.0, same)
+    MASK[...] = lax.dot_general(
+        PERM[...], same.astype(BF16), (((1,), (1,)), ((), ())), preferred_element_type=F32
+    )
+
     barrier = pltpu.get_barrier_semaphore()
 
     def greet(dev):
@@ -173,6 +190,12 @@
             for d in (0, 1):
                 hop(p, d, 1, h).start()
 
+    def rest(d, s):
+        block = zmod(z - (1 - 2 * d) * s)
+        return remote(WO.at[block], WP.at[block], rest_s.at[d, s], rest_r.at[d, s], partner)
+
+    rests = [(0, s) for s in range(H + 1)] + [(1, s) for s in range(1, H)]
+
     def step(p, s):
         for h in (0, 1):
             for d in (0, 1):
@@ -180,6 +203,9 @@
                     arrive(p, d, s, h)
                     if s < H - 1 or (s == H - 1 and d == h):
                         hop(p, d, s + 1, h).start()
+        if p == 2:
+            for d in range(2 if s < H else 1):
+                rest(d, s).start()
 
     def add(acc, w, block, first=False):
         product = dot(TOK[block], w[block])
@@ -206,6 +232,7 @@
             step(1, z_after[s])
         if s == H - 1:
             begin(2)
+            rest(0, 0).start()
         if s == relay_at:
             each(1, NE, relay)
         if s == tokens_at:
@@ -233,9 +260,7 @@
             if s + z_done <= H:
                 add_step(AZ, WZ, s + z_done)
 
-    row = lax.broadcasted_iota(jnp.int32, (T, T), 0)
-    col = lax.broadcasted_iota(jnp.int32, (T, T), 1)
-    perm = (col == lax.rem(row, 8) * J + lax.div(row, 8)).astype(F32).astype(BF16)
+    perm = PERM[...]
     XP[...] = dot(perm, AX[...].astype(BF16))
     rim = XP.at[pl.ds((J - 3) * 8, 24)]
     halo = remote(rim, HALO, halo_s, halo_r, at(e, zmod(z + 1), c))
@@ -251,7 +276,7 @@
     ext = jnp.concatenate(early + [XP[...]], 0)
     conv = conv_b[:, lane_c] + conv_w[3:4, lane_c] * ext[24:]
     for k in range(1, 4):
-        conv += conv_w[3 - k : 4 - k, lane_c] * ext[24 - 8 * k : 24 - 8 * k + T] * masks[:, k - 1 : k]
+        conv += conv_w[3 - k : 4 - k, lane_c] * ext[24 - 8 * k : 24 - 8 * k + T] * MASK[:, k - 1 : k]
     x_act = silu(conv).astype(BF16)
     XA[...] = x_act.astype(F32)
     PR[...] = dot(x_act, wxp[span(c, CH), :])
@@ -322,7 +347,17 @@
     delta = dot(PR[:, :R].astype(BF16), wdt[:, lane_c]) + dt_bias[:, lane_c]
     delta = jnp.maximum(delta, 0.0) + jnp.log1p(jnp.exp(-jnp.abs(delta)))
     DX[...] = delta * XA[...]
-    DD[...] = delta + (1.0 - masks[:, 0:1]) * FAR
+    DD[...] = delta + (1.0 - MASK[:, 0:1]) * FAR
+
+    def reach_send(i):
+        return remote(KS, SR.at[i], reach_s.at[i], reach_r.at[i], at(e, zmod(z + i + 1), c))
+
+    reach_sum = jnp.zeros((8, CH), F32)
+    for j in range(J):
+        reach_sum += DD[8 * j : 8 * j + 8, :]
+    KS[...] = jnp.broadcast_to(jnp.sum(reach_sum, axis=0, keepdims=True), (N, CH)).astype(BF16)
+    for i in range(near):
+        reach_send(i).start()
 
     slope = [rates[n : n + 1, lane_c] * (-LOG2E) for n in range(N)]
 
@@ -354,8 +389,7 @@
         HE[n] = jnp.where(top, 0.0, pltpu.roll(h, 1, 0))
         PE[n] = jnp.where(top, 1.0, pltpu.roll(p, 1, 0))
         states.append(h[7:8])
-    span_sum = jnp.broadcast_to(jnp.sum(reach, axis=0, keepdims=True), (N, CH))
-    KM[0] = jnp.concatenate(states + [span_sum], 0).astype(BF16)
+    KM[0] = jnp.concatenate(states, 0).astype(BF16)
 
     steep = rates[:, lane_c] * (-LOG2E)
 
@@ -365,36 +399,28 @@
             KM.at[0 if i < near else 1], KR.at[i], state_s.at[i], state_r.at[i],
             at(e, zmod(z + d), c),
         )
-
-    def join(earlier, latter):
-        both = latter.astype(F32)
-        h, reach = both[:N], both[N:]
-        if earlier is None:
-            return h, reach
-        return jnp.exp2(reach * steep) * earlier[0] + h, earlier[1] + reach
 
     for i in range(near):
         state_send(i).start()
     pump(5)
+    distance = jnp.zeros((N, CH), F32)
     for i in range(near):
+        reach_send(i).wait_recv()
         state_send(i).wait_recv()
-    entering = None
-    for i in range(near - 1, -1, -1):
-        entering = join(entering, KR[i])
+    entering = KR[near - 1].astype(F32)
+    for i in range(near - 2, -1, -1):
+        entering = jnp.exp2(SR[i].astype(F32) * steep) * entering + KR[i].astype(F32)
+    for i in range(near):
+        distance += SR[i].astype(F32)
     if far:
-        KM[1] = jnp.concatenate(entering, 0).astype(BF16)
-        for i in range(near, near + len(far)):
-            state_send(i).start()
+        KM[1] = entering.astype(BF16)
+        state_send(near).start()
         pump(6)
-        for i in range(near, near + len(far)):
-            state_send(i).wait_recv()
-        combined = None
-        for i in range(near + len(far) - 1, near - 1, -1):
-            combined = join(combined, KR[i])
-        entering = join(combined, KM[1])
+        state_send(near).wait_recv()
+        entering = jnp.exp2(distance * steep) * KR[near].astype(F32) + entering
     pump(7)
     for n in range(N):
-        HE[n] = HE[n] + PE[n] * entering[0][n : n + 1, :]
+        HE[n] = HE[n] + PE[n] * entering[n : n + 1, :]
 
     def correct(j, _):
         r = pl.ds(pl.multiple_of(j * 8, 8), 8)
@@ -411,49 +437,32 @@
     gate = silu(dot(perm, AZ[...].astype(BF16)))
     G[...] = dot(back, (Y[...] * gate).astype(BF16)).astype(BF16)
 
-    def swap(k):
-        return remote(XS.at[k], XR.at[k], swap_s.at[k], swap_r.at[k], partner)
+    gated = remote(G.at[span(o, TL)], GP, gate_s, gate_r, partner)
+    gated.start()
 
     def out_send(k):
         return remote(OS.at[k], RO.at[k], out_s.at[k], out_r.at[k], at(emod(e + k), z, c))
 
-    def group(low, high):
-        total = 2 * (high - low + 1) - (low == 0) - (high == H)
-
-        def offset(i):
-            i = lax.rem(i + e, total)
-            if low == 0:
-                return lax.div(i + 1, 2) * (1 - 2 * lax.rem(i, 2))
-            return (low + lax.div(i, 2)) * (1 - 2 * lax.rem(i, 2))
-
-        def multiply(i):
-            block = zmod(z + offset(i))
-            k = emod(block - e)
-            w = WO[block]
-            XS[k] = dot(G[span(o, TL), :], w).astype(BF16)
-            swap(k).start()
-            MO[k] = dot(G[span(c, TL), :], w)
-
-        def reduce(i):
-            k = emod(zmod(z + offset(i)) - e)
-            swap(k).wait_recv()
-            OS[k] = (MO[k] + XR[k].astype(F32)).astype(BF16)
-
-            @pl.when(k > 0)
-            def _():
-                out_send(k).start()
-
-        ahead = min(3, total)
-        each(0, ahead, multiply)
-
-        def both(i):
-            multiply(i)
-            reduce(i - ahead)
-
-        each(ahead, total, both)
-        each(total - ahead, total, reduce)
-
-    group(0, H)
+    def block_at(k):
+        return zmod(e + k)
+
+    def multiply(k):
+        MO[k] = dot(G[span(c, TL), :], WO[block_at(k)])
+
+    each(0, NE, multiply)
+    for d, s in rests:
+        rest(d, s).wait_recv()
+    gated.wait_recv()
+
+    def finish(k):
+        OS[k] = (MO[k] + dot(GP[...], WP[block_at(k)])).astype(BF16)
+
+    def finish_send(k):
+        finish(k)
+        out_send(k).start()
+
+    each(1, NE, finish_send)
+    finish(0)
     result = OS[0].astype(F32)
     for k in range(1, NE):
         out_send(k).wait_recv()
@@ -465,6 +474,8 @@
     halo.wait_send()
     for i in range(near + len(far)):
         state_send(i).wait_send()
+    for i in range(near):
+        reach_send(i).wait_send()
 
     def drain(k):
         tok_send(k).wait_send()
@@ -478,11 +489,10 @@
 
     everyone(drain_all)
 
-    def drain_pair(k):
-        tok_fwd(k).wait_send()
-        swap(k).wait_send()
-
-    each(0, NE, drain_pair)
+    each(0, NE, lambda k: tok_fwd(k).wait_send())
+    gated.wait_send()
+    for d, s in rests:
+        rest(d, s).wait_send()
 
     def drain_ring(s):
         for p in range(3):
@@ -506,12 +516,6 @@
     CH, OC, R, N = C2 // 2, w_out.shape[1], w_dt.shape[0], a_rate.shape[1]
     T, J, H = 2 * TL, TL // 4, NZ // 2
     PW = R + 128
-    z = lax.axis_index("fsdp") // 2
-    padded = jnp.concatenate([jnp.full((3,), -1, jnp.int32), segment_ids], 0)
-    window = lax.dynamic_slice_in_dim(padded, z * T, T + 3)
-    same = jnp.stack([window[3 - k : 3 - k + T] == window[3:] for k in (1, 2, 3)])
-    masks = same.reshape(3, 8, J).transpose(2, 1, 0).reshape(T, 3).astype(F32)
-    masks = jnp.pad(masks, ((0, 0), (0, 125)))
     wxp = jnp.pad(w_xproj, ((0, 0), (0, PW - w_xproj.shape[1])))
     near = min(H, 4)
     rounds = near + H // near - 1
@@ -531,6 +535,7 @@
             V((NZ, 2 * KR_, CH), BF16),
             V((NZ, 2 * KR_, CH), BF16),
             V((NZ, CH, 2 * OC), BF16),
+            V((NZ, CH, 2 * OC), BF16),
             V((T, CH), F32),
             V((T, CH), F32),
             V((T, CH), F32),
@@ -546,11 +551,14 @@
             V((T, CH), F32),
             V((N, 8, CH), F32),
             V((N, 8, CH), F32),
-            V((2, 2 * N, CH), BF16),
-            V((rounds, 2 * N, CH), BF16),
+            V((2, N, CH), BF16),
+            V((rounds, N, CH), BF16),
+            V((N, CH), BF16),
+            V((near, N, CH), BF16),
+            V((T, 8), F32),
+            V((T, T), BF16),
             V((T, CH), BF16),
-            V((NE, TL, DC), BF16),
-            V((NE, TL, DC), BF16),
+            V((TL, CH), BF16),
             V((NE, TL, DC), F32),
             V((NE, TL, DC), BF16),
             V((NE, TL, DC), BF16),
@@ -563,7 +571,9 @@
             dma((2, NE)), dma((2, NE)),
             dma((2, NE)), dma((2, NE)),
             dma((rounds,)), dma((rounds,)),
-            dma((NE,)), dma((NE,)),
+            dma((near,)), dma((near,)),
+            dma(()), dma(()),
+            dma((2, H + 1)), dma((2, H + 1)),
             dma((NE,)), dma((NE,)),
         ],
         compiler_params=pltpu.CompilerParams(
@@ -571,7 +581,7 @@
         ),
     )(
         tokens, w_in_x, w_in_z, w_out, conv_weight, conv_bias[None, :], wxp, w_dt,
-        dt_bias[None, :], a_rate.T, d_skip[None, :], masks,
+        dt_bias[None, :], a_rate.T, d_skip[None, :], segment_ids.reshape(NZ, T),
     )
 
 

time: 125 us -> 123 us (0.984); the launches traced: 125 us -> 120 us
  Pallas kernels: 121 us -> 117 us
    pallas_call x1, Pallas kernels: 121 us -> 117 us  [local(): pl.pallas_call(functools.partial(kernel, sizes), out_shape=jax.ShapeDtype...]
where the time goes in v4:
time: 123 us; the launch traced here: 120 us
  Pallas kernels  117 us (95%)
  local copies, waits for them, and re-layouts  3.27 us (3%)
    pallas_call x1, Pallas kernels, local(): pl.pallas_call(functools.partial(kernel, sizes), out_shape=jax.ShapeDtype...  117 us
    unnamed x24, local copies, waits for them, and re-layouts  3.22 us

profile of v4, /device:TPU:1, one launch (start us, length us, event | category | flops | bytes accessed | tf_op | source)
XLA Modules:
  0.0 120.5 jit_solution(1271092142278241469)
XLA Ops:
  0.0 1.2 copy.13
  1.2 0.0 copy-start.10
  1.2 0.0 copy-start
  1.2 0.0 copy-start.1
  1.2 0.0 copy-start.2
  1.2 0.0 copy-start.3
  1.2 0.0 copy-start.4
  1.2 0.0 copy-start.6
  1.3 0.6 copy-done.10
  1.9 0.0 copy-start.5
  1.9 0.0 copy-start.9
  1.9 0.0 copy-start.8
  1.9 0.0 copy-start.7
  1.9 0.2 copy-done
  2.1 0.0 copy-done.1
  2.2 0.1 copy-done.2
  2.2 0.1 copy-done.3
  2.3 0.0 copy-done.4
  2.3 0.0 copy-done.6
  2.3 0.4 copy-done.5
  2.7 0.0 copy-done.9
  2.7 0.0 copy-done.8
  2.7 0.0 copy-done.7
  2.7 117.1 %shard_map.118 = bf16[128,256]{1,0:T(8,128)(2,1)S(1)} custom-call(bf16[128,256]{1,0:T(8,128)(2,1)S(1)} %copy-done.4, bf16[128,512]{1,0:T(8,128)(2,1)S(1)} %copy-done.1, bf16[128,512]{1,0:T(8,128)(2,1)S(1)} %copy-done.2, bf16[512,128]{1,0:T(8,128)(2,1)S(1)} %copy-done.3, f32[4,512]{1,0:T(4,128)S(1)} %copy-done.6, f32[1,512]{1,0:T(1,128)S(1)} %bitcast.5, ...), custom_call_target="tpu_custom_call" | custom-call | tf_op jit(solution)/shard_map/pallas_call | solution.py:528
  119.8 0.6 copy.15
  (2 shorter events, 0.1 us)
Async XLA Ops:
  1.2 0.7 copy-start.10
  1.2 1.0 copy-start
  1.2 1.0 copy-start.1
  1.2 1.0 copy-start.2
  1.2 1.1 copy-start.3
  1.2 1.1 copy-start.4
  1.2 1.1 copy-start.6
  1.9 0.8 copy-start.5
  1.9 0.8 copy-start.9
  1.9 0.8 copy-start.8
  1.9 0.8 copy-start.7

commit v5 on v4

--- a/solution.py
+++ b/solution.py
@@ -221,7 +221,7 @@
         tok_fwd(k).start()
 
     relay_at, tokens_at = min(4, H - 1), min(7, H)
-    z_after = {2 * i + 1: i for i in range(1, H) if 2 * i + 1 < H}
+    z_after = {2 * i: i for i in range(1, H) if 2 * i < H}
     z_done = len(z_after)
     done = 0
     for s in range(1, H + 1):
@@ -265,6 +265,7 @@
     rim = XP.at[pl.ds((J - 3) * 8, 24)]
     halo = remote(rim, HALO, halo_s, halo_r, at(e, zmod(z + 1), c))
     halo.start()
+    pump(1)
     halo.wait_recv()
     lane_c = span(c, CH)
     top = lax.broadcasted_iota(jnp.int32, (8, CH), 0) == 0
@@ -285,11 +286,12 @@
     blank = [jnp.zeros((CR - 8 * L, 128), F32)] if CR > 8 * L else []
 
     def pack(q):
-        rows = span(q, 8)
+        rows = slice(8 * q, 8 * q + 8)
         tiles = [PR[rows, l * 128 : (l + 1) * 128] for l in range(L)]
         PB[q] = jnp.concatenate(tiles + blank, 0).astype(BF16)
 
-    each(0, 2 * NE, pack)
+    for q in range(2 * NE):
+        pack(q)
 
     def plane(k, rel):
         core = c if rel == 0 else o
@@ -340,9 +342,10 @@
     def unpack(q):
         chunk = GB[q].astype(F32)
         for l in range(L):
-            PR[span(q, 8), l * 128 : (l + 1) * 128] = chunk[8 * l : 8 * l + 8]
-
-    each(0, 2 * NE, unpack)
+            PR[8 * q : 8 * q + 8, l * 128 : (l + 1) * 128] = chunk[8 * l : 8 * l + 8]
+
+    for q in range(2 * NE):
+        unpack(q)
     pump(4)
     delta = dot(PR[:, :R].astype(BF16), wdt[:, lane_c]) + dt_bias[:, lane_c]
     delta = jnp.maximum(delta, 0.0) + jnp.log1p(jnp.exp(-jnp.abs(delta)))
@@ -377,7 +380,7 @@
         return later, reach
 
     zero = jnp.zeros((8, CH), F32)
-    ends, reach = lax.fori_loop(0, J, forward, ([zero] * N, zero))
+    ends, reach = lax.fori_loop(0, J, forward, ([zero] * N, zero), unroll=2)
     sub = lax.broadcasted_iota(jnp.int32, (8, CH), 0)
     states = []
     for n in range(N):
@@ -431,7 +434,7 @@
         Y[r, :] = y + d_skip[:, lane_c] * XA[r, :]
         return 0
 
-    lax.fori_loop(0, J, correct, 0)
+    lax.fori_loop(0, J, correct, 0, unroll=2)
     back = (col == lax.rem(row, J) * 8 + lax.div(row, J)).astype(F32).astype(BF16)
     pump(H)
     gate = silu(dot(perm, AZ[...].astype(BF16)))

time: 123 us -> 119 us (0.967)
  Pallas kernels: 117 us -> 113 us
    pallas_call x1, Pallas kernels: 117 us -> 113 us  [local(): pl.pallas_call(functools.partial(kernel, sizes), out_shape=jax.ShapeDtype...]
where the time goes in v5:
time: 119 us; the launch traced here: 117 us
  Pallas kernels  113 us (95%)
  local copies, waits for them, and re-layouts  3.27 us (3%)
    pallas_call x1, Pallas kernels, local(): pl.pallas_call(functools.partial(kernel, sizes), out_shape=jax.ShapeDtype...  113 us
    unnamed x24, local copies, waits for them, and re-layouts  3.22 us

profile of v5, /device:TPU:1, one launch (start us, length us, event | category | flops | bytes accessed | tf_op | source)
XLA Modules:
  0.0 116.7 jit_solution(5771950780709073736)
XLA Ops:
  0.0 1.2 %copy.13 = bf16[512,288]{1,0:T(8,128)(2,1)S(1)} copy(bf16[512,288]{0,1:T(8,128)(2,1)} %param.18) | data formatting | bytes 589824 | tf_op args[6]
  1.2 0.0 copy-start.10
  1.2 0.0 copy-start
  1.2 0.0 copy-start.1
  1.2 0.0 copy-start.2
  1.2 0.0 copy-start.3
  1.2 0.0 copy-start.4
  1.2 0.0 copy-start.6
  1.3 0.6 copy-done.10
  1.9 0.0 copy-start.5
  1.9 0.0 copy-start.9
  1.9 0.0 copy-start.8
  1.9 0.0 copy-start.7
  1.9 0.2 copy-done
  2.1 0.0 copy-done.1
  2.2 0.1 copy-done.2
  2.2 0.1 copy-done.3
  2.3 0.0 copy-done.4
  2.3 0.0 copy-done.6
  2.3 0.4 copy-done.5
  2.7 0.0 copy-done.9
  2.7 0.0 copy-done.8
  2.7 0.0 copy-done.7
  2.7 113.3 %shard_map.118 = bf16[128,256]{1,0:T(8,128)(2,1)S(1)} custom-call(bf16[128,256]{1,0:T(8,128)(2,1)S(1)} %copy-done.4, bf16[128,512]{1,0:T(8,128)(2,1)S(1)} %copy-done.1, bf16[128,512]{1,0:T(8,128)(2,1)S(1)} %copy-done.2, bf16[512,128]{1,0:T(8,128)(2,1)S(1)} %copy-done.3, f32[4,512]{1,0:T(4,128)S(1)} %copy-done.6, f32[1,512]{1,0:T(1,128)S(1)} %bitcast.5, ...), custom_call_target="tpu_custom_call" | custom-call | tf_op jit(solution)/shard_map/pallas_call | solution.py:531
  116.0 0.6 copy.15
  (2 shorter events, 0.1 us)
Async XLA Ops:
  1.2 0.7 copy-start.10
  1.2 1.0 copy-start
  1.2 1.0 copy-start.1
  1.2 1.0 copy-start.2
  1.2 1.1 copy-start.3
  1.2 1.1 copy-start.4
  1.2 1.1 copy-start.6
  1.9 0.8 copy-start.5
  1.9 0.8 copy-start.9
  1.9 0.8 copy-start.8
  1.9 0.8 copy-start.7

commit v6 on v5

--- a/solution.py
+++ b/solution.py
@@ -329,14 +329,14 @@
         each(1, NE, both)
 
     everyone(lambda k, rel: sum_send(k, rel).start())
-    pump(2)
+    pump(3)
     everyone(lambda k, rel: sum_send(k, rel).wait_recv())
     total = PB[mine].astype(F32)
     for k in range(1, 2 * NE):
         total += RB[k].astype(F32)
     GB[mine] = total.astype(BF16)
     everyone(lambda k, rel: all_send(k, rel).start())
-    pump(3)
+    pump(4)
     everyone(lambda k, rel: all_in(k, rel).wait_recv())
 
     def unpack(q):
@@ -380,7 +380,7 @@
         return later, reach
 
     zero = jnp.zeros((8, CH), F32)
-    ends, reach = lax.fori_loop(0, J, forward, ([zero] * N, zero), unroll=2)
+    ends, reach = lax.fori_loop(0, J, forward, ([zero] * N, zero), unroll=4)
     sub = lax.broadcasted_iota(jnp.int32, (8, CH), 0)
     states = []
     for n in range(N):
@@ -434,7 +434,7 @@
         Y[r, :] = y + d_skip[:, lane_c] * XA[r, :]
         return 0
 
-    lax.fori_loop(0, J, correct, 0, unroll=2)
+    lax.fori_loop(0, J, correct, 0, unroll=4)
     back = (col == lax.rem(row, J) * 8 + lax.div(row, J)).astype(F32).astype(BF16)
     pump(H)
     gate = silu(dot(perm, AZ[...].astype(BF16)))

time: 119 us -> 119 us (level); the launches traced: 117 us -> 119 us
  Pallas kernels: 113 us -> 116 us
    pallas_call x1, Pallas kernels: 113 us -> 116 us  [local(): pl.pallas_call(functools.partial(kernel, sizes), out_shape=jax.ShapeDtype...]
where the time goes in v6:
time: 119 us
  Pallas kernels  116 us (97%)
  local copies, waits for them, and re-layouts  3.27 us (3%)
    pallas_call x1, Pallas kernels, local(): pl.pallas_call(functools.partial(kernel, sizes), out_shape=jax.ShapeDtype...  116 us
    unnamed x24, local copies, waits for them, and re-layouts  3.22 us

profile of v6, /device:TPU:1, one launch (start us, length us, event | category | flops | bytes accessed | tf_op | source)
XLA Modules:
  0.0 118.9 jit_solution(3904323895537445107)
XLA Ops:
  0.0 1.2 copy.13
  1.2 0.0 copy-start.10
  1.2 0.0 copy-start
  1.2 0.0 copy-start.1
  1.2 0.0 copy-start.2
  1.2 0.0 copy-start.3
  1.2 0.0 copy-start.4
  1.2 0.0 copy-start.6
  1.3 0.6 copy-done.10
  1.9 0.0 copy-start.5
  1.9 0.0 copy-start.9
  1.9 0.0 copy-start.8
  1.9 0.0 copy-start.7
  1.9 0.2 copy-done
  2.1 0.0 copy-done.1
  2.2 0.1 copy-done.2
  2.2 0.1 copy-done.3
  2.3 0.0 copy-done.4
  2.3 0.0 copy-done.6
  2.3 0.4 copy-done.5
  2.7 0.0 copy-done.9
  2.7 0.0 copy-done.8
  2.7 0.0 copy-done.7
  2.7 115.6 %shard_map.118 = bf16[128,256]{1,0:T(8,128)(2,1)S(1)} custom-call(bf16[128,256]{1,0:T(8,128)(2,1)S(1)} %copy-done.4, bf16[128,512]{1,0:T(8,128)(2,1)S(1)} %copy-done.1, bf16[128,512]{1,0:T(8,128)(2,1)S(1)} %copy-done.2, bf16[512,128]{1,0:T(8,128)(2,1)S(1)} %copy-done.3, f32[4,512]{1,0:T(4,128)S(1)} %copy-done.6, f32[1,512]{1,0:T(1,128)S(1)} %bitcast.5, ...), custom_call_target="tpu_custom_call" | custom-call | tf_op jit(solution)/shard_map/pallas_call | solution.py:531
  118.3 0.6 copy.15
  (2 shorter events, 0.1 us)
Async XLA Ops:
  1.2 0.7 copy-start.10
  1.2 1.0 copy-start
  1.2 1.0 copy-start.1
  1.2 1.0 copy-start.2
  1.2 1.1 copy-start.3
  1.2 1.1 copy-start.4
  1.2 1.1 copy-start.6
  1.9 0.8 copy-start.5
  1.9 0.8 copy-start.9
  1.9 0.8 copy-start.8
  1.9 0.8 copy-start.7
